TPU v7x, 128 devices: a whole 4x4x4 slice. The times are simulated.
128 devices in a mesh: row: 8 (over z_lo, y), col: 16 (over z_hi, x, core).
Axes of the slice: x: 4, y: 4, z: 4 (z_hi: 2, z_lo: 2; z = z_hi * 2 + z_lo), core: 2. Of those that a mesh axis runs over, the one named last changes fastest.
Arguments:
- records: bfloat16 [2048, 19200], P(None, ('row', 'col')), may hold values from -40 to 40
- assignment: int32 [2048], replicated, may hold values from 0 to 2047, each once
- channel_flags: int32 [32, 2048], replicated, may hold values from 0 to 1, as said below
Outputs:
- correlations: bfloat16 [2048, 2048, 256], P('row', 'col')
Inputs may be any that keep to these rules, and one draw needn't show every extreme that they name: `channel_flags`: exactly 16 channels are bad in every window.
All inputs are finite; a program needn't handle non-finite values.
Results may differ from a plain program's by a relative error of at most 0.0066.
Values may be sent and summed in bfloat16 or wider, within the bound.
No kernel may reach another device: no remote copies, remote signals or barrier semaphores. Data moves between devices by JAX's collectives and lax.ppermute only.
A program may use at most 192 MiB of HBM per device.

v0:
```python
import math

import jax
import jax.numpy as jnp
import numpy as np
from jax import lax
from jax.experimental import pallas as pl
from jax.experimental.pallas import tpu as pltpu
from jax.sharding import PartitionSpec as P

SAMPLES = 600
NFFT = 1024
FIRST_BIN = 10
BINS = 256
MAX_LAG = 128
WINDOWS = 32
CHANS = 2048
GROUP = 16
SLICE = 150
QUARTERS = 4
KGS = 64
PITCH = 264

f32 = jnp.float32
bf16 = jnp.bfloat16
vmem = pl.BlockSpec(memory_space=pltpu.VMEM)
smem = pl.BlockSpec(memory_space=pltpu.SMEM)
anym = pl.BlockSpec(memory_space=pl.ANY)


def forward_table():
    phase = (FIRST_BIN + np.arange(BINS))[None, :] * np.arange(SAMPLES)[:, None] % NFFT
    angle = 2.0 * math.pi / NFFT * phase
    table = np.concatenate([np.cos(angle), -np.sin(angle)], axis=1)
    return jnp.asarray(table.reshape(QUARTERS, SLICE, 2 * BINS), bf16)


def lag_table():
    phase = (FIRST_BIN + np.arange(BINS))[None, :] * (np.arange(2 * MAX_LAG) - MAX_LAG)[:, None] % NFFT
    angle = 2.0 * math.pi / NFFT * phase
    table = np.concatenate([np.cos(angle), -np.sin(angle)], axis=1)
    return jnp.asarray(jnp.asarray(table, bf16).astype(f32) / math.sqrt(BINS), bf16)


def order_channels(records_t, assignment):
    block = 512

    def kernel(assign_hbm, rec_hbm, out_ref, assign_ref, rec_ref, turn_ref, sems):
        assign_in = pltpu.make_async_copy(assign_hbm, assign_ref, sems.at[0])
        rec_in = pltpu.make_async_copy(rec_hbm, rec_ref, sems.at[1])
        assign_in.start()
        rec_in.start()
        assign_in.wait()
        chan = lax.broadcasted_iota(jnp.int32, (CHANS, block), 0)
        for n in range(CHANS // block):
            at = slice(n * block, (n + 1) * block)
            onehot = (chan == assign_ref[:, at]).astype(f32).astype(bf16)
            if n == 0:
                rec_in.wait()
            turn_ref[n, 0:SLICE, :] = jnp.dot(rec_ref[...], onehot, preferred_element_type=f32)
            out_ref[at, :] = turn_ref[n].T[:, :SLICE].astype(bf16)

    return pl.pallas_call(
        kernel,
        out_shape=jax.ShapeDtypeStruct((CHANS, SLICE), bf16),
        in_specs=[anym, anym],
        out_specs=vmem,
        scratch_shapes=[
            pltpu.VMEM((1, CHANS), jnp.int32),
            pltpu.VMEM((SLICE, CHANS), bf16),
            pltpu.VMEM((CHANS // block, 256, block), f32),
            pltpu.SemaphoreType.DMA((2,)),
        ],
        compiler_params=pltpu.CompilerParams(vmem_limit_bytes=58 * 2**20),
    )(assignment.reshape(1, CHANS), records_t)


def whiten(slices, keep, table):
    def kernel(x_ref, keep_ref, f_ref, out_ref, again_ref, z0, z1, z2, z3, turn_ref, sem):
        zs = [z0, z1, z2, z3]
        spec = None
        for quarter in range(QUARTERS):
            rows = jnp.concatenate([x_ref[QUARTERS * w + quarter] for w in range(WINDOWS)], axis=0)
            part = jnp.dot(rows, f_ref[quarter], preferred_element_type=f32)
            spec = part if spec is None else spec + part
        re, im = spec[:, :BINS], spec[:, BINS:]
        power = re * re + im * im
        water = jnp.mean(power, axis=1, keepdims=True)
        padded = jnp.concatenate([power, jnp.zeros((512, 128), f32)], axis=1)
        total = padded + pltpu.roll(padded, 1, 1)
        total = total + pltpu.roll(total, 2, 1)
        total = total + pltpu.roll(total, 4, 1)
        total = total + pltpu.roll(padded, 8, 1)
        smooth = pltpu.roll(total, 384 - 4, 1)[:, :BINS]
        amp = lax.rsqrt(smooth / 9.0 + 0.1 * water + 1e-6) * keep_ref[...]
        for h in range(4):
            zs[h][...] = spec[:, h * 128 : (h + 1) * 128] * amp[:, (h % 2) * 128 : (h % 2) * 128 + 128]
        low = lax.broadcasted_iota(jnp.int32, (WINDOWS, 128), 1) < 64
        for ri in range(2):
            for pair in range(GROUP // 2):
                rows = []
                for h in range(2):
                    first = zs[2 * ri + h][pl.ds(2 * pair, WINDOWS, stride=GROUP), :]
                    second = zs[2 * ri + h][pl.ds(2 * pair + 1, WINDOWS, stride=GROUP), :]
                    rows.append(jnp.where(low, first, pltpu.roll(second, 64, 1)))
                    rows.append(jnp.where(low, pltpu.roll(first, 64, 1), second))
                turned = jnp.concatenate(rows, axis=0).T
                for j in range(2):
                    turn_ref[pl.ds(ri * GROUP + 2 * pair + j, KGS, stride=2 * GROUP), :] = turned[
                        j * KGS : (j + 1) * KGS
                    ]
        out_ref[...] = turn_ref[...].astype(bf16)
        copy = pltpu.make_async_copy(out_ref, again_ref, sem)
        copy.start()
        copy.wait()

    outs = pl.pallas_call(
        kernel,
        out_shape=[jax.ShapeDtypeStruct((KGS * 2 * GROUP, 128), bf16)] * 2,
        in_specs=[vmem] * 3,
        out_specs=[vmem, anym],
        scratch_shapes=[pltpu.VMEM((512, 128), f32)] * 4
        + [pltpu.VMEM((KGS * 2 * GROUP, 128), f32), pltpu.SemaphoreType.DMA],
        compiler_params=pltpu.CompilerParams(vmem_limit_bytes=40 * 2**20),
    )(slices, keep, table)
    return [out.reshape(KGS, 2, GROUP, 128) for out in outs]


def after(arrays, others):
    count = len(arrays)
    return pl.pallas_call(
        lambda *refs: None,
        out_shape=[jax.ShapeDtypeStruct(a.shape, a.dtype) for a in arrays],
        in_specs=[anym] * (count + len(others)),
        out_specs=[anym] * count,
        input_output_aliases={n: n for n in range(count)},
        cost_estimate=pl.CostEstimate(flops=0, bytes_accessed=0, transcendentals=0),
    )(*arrays, *others)


def pair_chunk(blocks, places, second, scale, table, result):
    count = len(blocks)
    group = 4
    rows = group * GROUP

    def kernel(*refs):
        place_ref, scale_ref, tab_ref = refs[:3]
        out_hbm, held, spec_re, spec_im, stage, in_sems, sems = refs[-7:]
        half = KGS // 2

        def copy_in(n, h):
            at = pl.ds(h * half, half)
            return pltpu.make_async_copy(refs[3 + n].at[at], held.at[n, at], in_sems.at[n, h])

        def copy_out(b):
            at = pl.multiple_of(place_ref[b] * GROUP, GROUP)
            return pltpu.make_async_copy(stage.at[b], out_hbm.at[pl.ds(at, GROUP)], sems.at[b])

        for h in range(2):
            for n in range(8 + group):
                copy_in(n, h).start()
        for n in range(8 + group, 8 + count):
            for h in range(2):
                copy_in(n, h).start()
        lane = lax.broadcasted_iota(jnp.int32, (rows, 256), 1) % 128 // 32
        columns = [pl.multiple_of(place_ref[count + b] * GROUP, GROUP) for b in range(8)]

        @pl.loop(0, count // group)
        def _(turn):
            base = turn * group
            starts = [pl.multiple_of(place_ref[base + b] * GROUP, GROUP) for b in range(group)]
            scales = jnp.concatenate([scale_ref[pl.ds(at, GROUP), :] for at in starts], axis=0)

            @pl.loop(0, 2)
            def _(h):
                @pl.when(turn == 0)
                def _():
                    for n in range(8 + group):
                        copy_in(n, h).wait()

                @pl.when(turn > 0)
                def _():
                    for n in range(8 + group, 8 + count):
                        copy_in(n, h).wait()

                @pl.loop(0, half, unroll=half)
                def _(i):
                    kg = h * half + i
                    vr, vi = [jnp.concatenate([held[b, kg, ri] for b in range(8)], axis=0) for ri in range(2)]
                    rhs = jnp.concatenate(
                        [jnp.concatenate([vr, vi], axis=1), jnp.concatenate([-vi, vr], axis=1)], axis=0
                    )
                    lhs = jnp.concatenate(
                        [
                            jnp.concatenate([held[8 + base + b, kg, ri] for b in range(group)], axis=0)
                            for ri in range(2)
                        ],
                        axis=1,
                    )
                    lhs = jnp.concatenate(
                        [jnp.where(lane == ki, lhs, jnp.zeros_like(lhs)) for ki in range(4)], axis=0
                    )
                    cross = lax.dot_general(lhs, rhs, (((1,), (1,)), ((), ())), preferred_element_type=f32)
                    for ki in range(4):
                        part = cross[ki * rows : (ki + 1) * rows]
                        spec_re[pl.ds(ki * KGS + kg, rows, stride=PITCH), :] = part[:, :128] * scales
                        spec_im[pl.ds(ki * KGS + kg, rows, stride=PITCH), :] = part[:, 128:] * scales

            @pl.loop(0, group // 2)
            def _(couple):
                for i in range(GROUP):
                    b = 2 * couple + i // (GROUP // 2)
                    row = 2 * (i % (GROUP // 2))
                    halves = []
                    for ref in (spec_re, spec_im):
                        at = [pl.multiple_of((b * GROUP + row + j) * PITCH, 8) for j in range(2)]
                        halves.append(
                            jnp.concatenate([ref[pl.ds(a, BINS), :].astype(bf16) for a in at], axis=1)
                        )
                    lagged = lax.dot_general(
                        jnp.concatenate(halves, axis=0),
                        tab_ref[...],
                        (((0,), (1,)), ((), ())),
                        preferred_element_type=f32,
                    ).astype(bf16)
                    for j in range(2):
                        for c in range(8):
                            at = j * 128 + c * GROUP
                            stage[base + b, row + j, pl.ds(columns[c], GROUP), :] = lagged[at : at + GROUP]
                for b in range(2):
                    copy_out(base + 2 * couple + b).start()

        for b in range(count):
            copy_out(b).wait()

    ins = [places, scale, table, *second, *blocks]
    specs = [smem, vmem, vmem] + [anym] * (8 + count)
    aliases = {}
    if result is not None:
        aliases = {len(ins): 0}
        ins.append(result)
        specs.append(anym)
    return pl.pallas_call(
        kernel,
        out_shape=jax.ShapeDtypeStruct((256, 128, 2 * MAX_LAG), bf16),
        in_specs=specs,
        out_specs=anym,
        scratch_shapes=[
            pltpu.VMEM((8 + count, KGS, 2, GROUP, 128), bf16),
            pltpu.VMEM((rows * PITCH, 128), f32),
            pltpu.VMEM((rows * PITCH, 128), f32),
            pltpu.VMEM((count, GROUP, 128, 2 * MAX_LAG), bf16),
            pltpu.SemaphoreType.DMA((8 + count, 2)),
            pltpu.SemaphoreType.DMA((count,)),
        ],
        input_output_aliases=aliases,
        compiler_params=pltpu.CompilerParams(vmem_limit_bytes=58 * 2**20),
        cost_estimate=pl.CostEstimate(flops=15 * 10**9, bytes_accessed=10 * 2**20, transcendentals=0),
    )(*ins)


def col_perm(dz, dx, dcore):
    def to(i):
        z, x, core = i // 8, i // 2 % 4, i % 2
        return ((z ^ dz) * 4 + (x + dx) % 4) * 2 + (core ^ dcore)

    return [(i, to(i)) for i in range(16)]


def row_perm(dz, dy):
    return [(i, (i // 4 ^ dz) * 4 + (i % 4 + dy) % 4) for i in range(8)]


def per_device(records, assignment, channel_flags):
    row = lax.axis_index("row")
    col = lax.axis_index("col")
    layout = assignment.reshape(8, 16, GROUP)
    z_lo, y = row // 4, row % 4
    z_hi, x, core = col // 8, col // 2 % 4, col % 2
    steps = (0, -1, 1, 2)
    second_places = [(z_lo ^ dz) * 4 + (y + d) % 4 for dz in range(2) for d in steps]
    row_chans = lax.dynamic_index_in_dim(layout, row, 0, keepdims=False).reshape(-1)
    col_layout = lax.dynamic_index_in_dim(layout, col, 1, keepdims=False)
    col_chans = jnp.take(col_layout, jnp.stack(second_places), axis=0, mode="clip").reshape(-1)
    own_row = lax.dynamic_index_in_dim(layout, row, 0, keepdims=False)
    own_chans = lax.dynamic_index_in_dim(own_row, col, 0, keepdims=False)

    ordered = order_channels(records.T, assignment)
    slices = lax.all_to_all(
        ordered.reshape(128, GROUP, SLICE), ("row", "col"), split_axis=0, concat_axis=0, tiled=True
    )

    flags = channel_flags.astype(f32)
    row_flags = jnp.take(flags, row_chans, axis=1, mode="clip")
    col_flags = jnp.take(flags, col_chans, axis=1, mode="clip")
    keep = jnp.take(flags, own_chans, axis=1, mode="clip").reshape(WINDOWS * GROUP, 1)
    shared = jnp.dot(jnp.transpose(row_flags), col_flags, precision=lax.Precision.HIGHEST)
    scale = lax.rsqrt(jnp.maximum(shared, 1.0))

    places = [
        jnp.stack(
            [((z_hi ^ dz) * 4 + (x + d) % 4) * 2 + (core ^ dc) for dc in range(2) for d in steps] + second_places
        ).astype(jnp.int32)
        for dz in range(2)
    ]
    slices, keep, scale, places = lax.optimization_barrier((slices, keep, scale, places))
    own, again = whiten(slices, keep, forward_table())

    y_up, y_down = row_perm(0, 1), row_perm(0, -1)
    x_up, x_down, flip = col_perm(0, 1, 0), col_perm(0, -1, 0), col_perm(0, 0, 1)

    def along_row(block, perm, name):
        with jax.named_scope(name):
            return lax.ppermute(block, "row", perm)

    def along_col(block, perm, name):
        with jax.named_scope(name):
            return lax.ppermute(block, "col", perm)

    zl = along_row(own, row_perm(1, 0), "zl")
    y_below, y_above = along_row(own, y_up, "y_below"), along_row(own, y_down, "y_above")
    x_below, x_above = along_col(own, x_up, "x_below"), along_col(own, x_down, "x_above")

    (again,) = after([again], [zl, y_below, y_above])
    zl_below, zl_above = along_row(zl, y_up, "zl_below"), along_row(zl, y_down, "zl_above")
    zh = along_col(again, col_perm(1, 0, 0), "zh")
    x_far = along_col(x_below, x_up, "x_far")
    x_far_other = along_col(x_above, col_perm(0, -1, 1), "x_far_other")

    (y_below,) = after([y_below], [zl_below])
    y_far, zl_far = along_row(y_below, y_up, "y_far"), along_row(zl_above, y_down, "zl_far")
    zh_below, zh_above = along_col(zh, x_up, "zh_below"), along_col(zh, x_down, "zh_above")
    zh_far = along_col(x_far, col_perm(1, 0, 0), "zh_far")
    again, x_below, x_above = after([again, x_below, x_above], [y_far, zl_far, zh, x_far, x_far_other])
    swaps = [along_col(block, flip, "core_swap") for block in (again, x_below, x_above)]

    second = [own, y_below, y_above, y_far, zl, zl_below, zl_above, zl_far]
    table = lag_table()
    blocks = [own, x_below, x_above, x_far, *swaps, x_far_other]
    result = pair_chunk(blocks, places[0], second, scale, table, None)
    blocks = after([zh, zh_below, zh_above, zh_far], [result])
    blocks = [*blocks, *(along_col(block, flip, "core_swap") for block in blocks)]
    result = pair_chunk(blocks, places[1], second, scale, table, result)
    return result


def solution(mesh):
    placed = (P(None, ("row", "col")), P(), P())
    return jax.shard_map(
        per_device, mesh=mesh, in_specs=placed, out_specs=P("row", "col", None), check_vma=False
    )
```

profile of v0, /device:TPU:1, one launch (start us, length us, event | category | flops | bytes accessed | tf_op | source)
XLA Modules:
  0.0 132.5 jit_solution(6320794194306584527)
XLA Ops:
  0.0 4.2 %shard_map.55 = bf16[2048,150]{1,0:T(8,128)(2,1)} custom-call(s32[1,2048]{1,0:T(1,128)} %bitcast.48, bf16[150,2048]{1,0:T(8,128)(2,1)} %bitcast.45), custom_call_target="tpu_custom_call" | custom-call | tf_op jit(solution)/shard_map/pallas_call | solution.py:63
  4.2 11.5 %all-to-all-start = ((bf16[128,16,150]{2,1,0:T(8,128)(2,1)}), bf16[128,16,150]{2,1,0:T(8,128)(2,1)S(1)}, u32[]{:S(2)}, u32[]{:S(2)}) async-start(bf16[128,16,150]{2,1,0:T(8,128)(2,1)} %bitcast.44), calls=%async_computation | async-start | bytes 2097152 | tf_op jit(solution)/shard_map/all_to_all | solution.py:289
  17.6 1.3 copy.18
  22.4 0.9 fusion.refs_1_
  23.3 11.4 %all-to-all-done.x_ref = bf16[128,16,150]{2,1,0:T(8,128)(2,1)S(1)} async-done(((bf16[128,16,150]{2,1,0:T(8,128)(2,1)}), bf16[128,16,150]{2,1,0:T(8,128)(2,1)S(1)}, u32[]{:S(2)}, u32[]{:S(2)}) %all-to-all-start) | async-done | bytes 614432 | tf_op jit(solution)/shard_map/all_to_all | solution.py:289
  34.9 1.1 copy-done.1
  36.0 3.7 %shard_map.56 = (bf16[2048,128]{1,0:T(8,128)(2,1)S(1)}, bf16[2048,128]{1,0:T(8,128)(2,1)S(1)}) custom-call(bf16[128,16,150]{2,1,0:T(8,128)(2,1)S(1)} %all-to-all-done.x_ref, f32[512,1]{1,0:T(8,128)S(1)} %copy.20.keep_ref, bf16[4,150,512]{2,1,0:T(8,128)(2,1)S(1)} %copy-done.1), custom_call_target="tpu_custom_call" | custom-call | tf_op jit(solution)/shard_map/pallas_call | solution.py:117
  42.4 1.2 collective-permute-start.13
  43.8 9.0 %collective-permute-done.1.refs_1_.refs_7_ = bf16[64,2,16,128]{3,2,1,0:T(8,128)(2,1)S(1)} collective-permute-done((bf16[64,2,16,128]{3,2,1,0:T(8,128)(2,1)S(1)}, bf16[64,2,16,128]{3,2,1,0:T(8,128)(2,1)S(1)}, u32[]{:S(2)}, u32[]{:S(2)}) %collective-permute-start.1) | collective-permute-done | bytes 524320 | tf_op jit(solution)/shard_map/zl/ppermute | solution.py:314
  55.5 2.7 %collective-permute-start.7 = (bf16[64,2,16,128]{3,2,1,0:T(8,128)(2,1)}, bf16[64,2,16,128]{3,2,1,0:T(8,128)(2,1)S(1)}, u32[]{:S(2)}, u32[]{:S(2)}) collective-permute-start(bf16[64,2,16,128]{3,2,1,0:T(8,128)(2,1)} %shard_map.58.refs_0_), channel_id=1, source_target_pairs={{0,8},{1,9},{2,10},{3,11},{4,12},{5,13},{6,14},{7,15},{8,0},{9,1},... | collective-permute-start | bytes 1572872 | tf_op jit(solution)/shard_map/zh/ppermute | solution.py:318
  58.2 2.7 %collective-permute-start.14 = (bf16[64,2,16,128]{3,2,1,0:T(8,128)(2,1)}, bf16[64,2,16,128]{3,2,1,0:T(8,128)(2,1)S(1)}, u32[]{:S(2)}, u32[]{:S(2)}) collective-permute-start(bf16[64,2,16,128]{3,2,1,0:T(8,128)(2,1)} %collective-permute-done.13.refs_2_), channel_id=1, source_target_pairs={{0,7},{1,6},{2,1},{3,0},{4,3},{5,2},{6,5},{7,4},{8,15},{9,14},{10,... | collective-permute-start | bytes 1572872 | tf_op jit(solution)/shard_map/x_far_other/ppermute | solution.py:318
  61.5 2.8 %collective-permute-done.5.refs_9_ = bf16[64,2,16,128]{3,2,1,0:T(8,128)(2,1)} collective-permute-done((bf16[64,2,16,128]{3,2,1,0:T(8,128)(2,1)S(1)}, bf16[64,2,16,128]{3,2,1,0:T(8,128)(2,1)}, u32[]{:S(2)}, u32[]{:S(2)}) %collective-permute-start.5) | collective-permute-done | bytes 524320 | tf_op jit(solution)/shard_map/zl_above/ppermute | solution.py:314
  64.4 1.8 %collective-permute-start.6 = (bf16[64,2,16,128]{3,2,1,0:T(8,128)(2,1)}, bf16[64,2,16,128]{3,2,1,0:T(8,128)(2,1)S(1)}, u32[]{:S(2)}, u32[]{:S(2)}) collective-permute-start(bf16[64,2,16,128]{3,2,1,0:T(8,128)(2,1)} %collective-permute-done.5.refs_9_), channel_id=1, source_target_pairs={{0,48},{16,0},{32,16},{48,32},{64,112},{80,64},{96,80},{112,96},{1... | collective-permute-start | bytes 1572872 | tf_op jit(solution)/shard_map/zl_far/ppermute | solution.py:314
  67.0 5.6 %collective-permute-done.14.refs_7_.refs_18_ = bf16[64,2,16,128]{3,2,1,0:T(8,128)(2,1)S(1)} collective-permute-done((bf16[64,2,16,128]{3,2,1,0:T(8,128)(2,1)}, bf16[64,2,16,128]{3,2,1,0:T(8,128)(2,1)S(1)}, u32[]{:S(2)}, u32[]{:S(2)}) %collective-permute-start.14) | collective-permute-done | bytes 524320 | tf_op jit(solution)/shard_map/x_far_other/ppermute | solution.py:318
  72.6 3.5 %collective-permute-done.11.refs_6_.refs_14_ = bf16[64,2,16,128]{3,2,1,0:T(8,128)(2,1)} collective-permute-done((bf16[64,2,16,128]{3,2,1,0:T(8,128)(2,1)}, bf16[64,2,16,128]{3,2,1,0:T(8,128)(2,1)}, u32[]{:S(2)}, u32[]{:S(2)}) %collective-permute-start.11) | collective-permute-done | bytes 524320 | tf_op jit(solution)/shard_map/x_far/ppermute | solution.py:318
  76.1 2.6 %collective-permute-done.4.refs_3_.refs_6_ = bf16[64,2,16,128]{3,2,1,0:T(8,128)(2,1)S(1)} collective-permute-done((bf16[64,2,16,128]{3,2,1,0:T(8,128)(2,1)}, bf16[64,2,16,128]{3,2,1,0:T(8,128)(2,1)S(1)}, u32[]{:S(2)}, u32[]{:S(2)}) %collective-permute-start.4) | collective-permute-done | bytes 524320 | tf_op jit(solution)/shard_map/y_far/ppermute | solution.py:314
  79.5 4.1 %collective-permute-start.15 = (bf16[64,2,16,128]{3,2,1,0:T(8,128)(2,1)}, bf16[64,2,16,128]{3,2,1,0:T(8,128)(2,1)S(1)}, u32[]{:S(2)}, u32[]{:S(2)}) collective-permute-start(bf16[64,2,16,128]{3,2,1,0:T(8,128)(2,1)} %get-tuple-element.28), channel_id=1, source_target_pairs={{0,1},{1,0},{2,3},{3,2},{4,5},{5,4},{6,7},{7,6},{8,9},{9,8},{10,11... | collective-permute-start | bytes 1572872 | tf_op jit(solution)/shard_map/core_swap/ppermute | solution.py:318
  84.1 3.9 %collective-permute-start.12 = (bf16[64,2,16,128]{3,2,1,0:T(8,128)(2,1)}, bf16[64,2,16,128]{3,2,1,0:T(8,128)(2,1)S(1)}, u32[]{:S(2)}, u32[]{:S(2)}) collective-permute-start(bf16[64,2,16,128]{3,2,1,0:T(8,128)(2,1)} %collective-permute-done.11.refs_6_.refs_14_), channel_id=1, source_target_pairs={{0,8},{1,9},{2,10},{3,11},{4,12},{5,13},{6,14},{7,15},{8,0},{9,1},... | collective-permute-start | bytes 1572872 | tf_op jit(solution)/shard_map/zh_far/ppermute | solution.py:318
  88.0 1.5 %collective-permute-start.8 = (bf16[64,2,16,128]{3,2,1,0:T(8,128)(2,1)}, bf16[64,2,16,128]{3,2,1,0:T(8,128)(2,1)S(1)}, u32[]{:S(2)}, u32[]{:S(2)}) collective-permute-start(bf16[64,2,16,128]{3,2,1,0:T(8,128)(2,1)} %copy-done.4), channel_id=1, source_target_pairs={{0,2},{1,3},{2,4},{3,5},{4,6},{5,7},{6,0},{7,1},{8,10},{9,11},{10,... | collective-permute-start | bytes 1572872 | tf_op jit(solution)/shard_map/zh_below/ppermute | solution.py:318
  90.2 0.8 copy-done.20
  91.1 17.0 %shard_map.60.refs_4_.refs_19_ = bf16[256,128,256]{2,1,0:T(8,128)(2,1)} custom-call(s32[16]{0:T(128)} %stack.114.refs_0_, f32[256,128]{1,0:T(8,128)} %fusion.refs_1_, bf16[256,512]{1,0:T(8,128)(2,1)} %constant.178.refs_2_, bf16[64,2,16,128]{3,2,1,0:T(8,128)(2,1)} %bitcast.41, bf16[64,2,16,128]{3,2,1,0:T(8,128)(2,1)} %shard_map.57.refs_4_, ...), custom_call_target="tpu_custom_call" | custom-call | flops 15000000512 | bytes 10485760 | tf_op jit(solution)/shard_map/pallas_call | solution.py:243
  109.9 0.8 collective-permute-start.18
  111.3 1.2 collective-permute-done.18.refs_15_
  115.6 16.7 %shard_map.62 = bf16[256,128,256]{2,1,0:T(8,128)(2,1)} custom-call(s32[16]{0:T(128)} %stack.123.refs_0_, f32[256,128]{1,0:T(8,128)} %fusion.refs_1_, bf16[256,512]{1,0:T(8,128)(2,1)} %constant.178.refs_2_, bf16[64,2,16,128]{3,2,1,0:T(8,128)(2,1)} %bitcast.43, bf16[64,2,16,128]{3,2,1,0:T(8,128)(2,1)} %shard_map.57.refs_4_, ...), custom_call_target="tpu_custom_call", output_to_operand_aliasing={{}: (19, {})} | custom-call | flops 15000000512 | bytes 10485760 | tf_op jit(solution)/shard_map/pallas_call | solution.py:243
  (95 shorter events, 19.8 us)
Async XLA Ops:
  4.2 30.6 %all-to-all-start = ((bf16[128,16,150]{2,1,0:T(8,128)(2,1)}), bf16[128,16,150]{2,1,0:T(8,128)(2,1)S(1)}, u32[]{:S(2)}, u32[]{:S(2)}) async-start(bf16[128,16,150]{2,1,0:T(8,128)(2,1)} %bitcast.44), calls=%async_computation | async-start | bytes 2097152 | tf_op jit(solution)/shard_map/all_to_all | solution.py:289
  40.5 48.9 %copy-start.2 = (bf16[2048,128]{1,0:T(8,128)(2,1)}, bf16[2048,128]{1,0:T(8,128)(2,1)S(1)}, u32[]{:S(2)}) copy-start(bf16[2048,128]{1,0:T(8,128)(2,1)S(1)} %get-tuple-element.23) | copy-start | bytes 1572868
  40.5 12.3 %collective-permute-start.1 = (bf16[64,2,16,128]{3,2,1,0:T(8,128)(2,1)S(1)}, bf16[64,2,16,128]{3,2,1,0:T(8,128)(2,1)S(1)}, u32[]{:S(2)}, u32[]{:S(2)}) collective-permute-start(bf16[64,2,16,128]{3,2,1,0:T(8,128)(2,1)S(1)} %bitcast.36), channel_id=1, source_target_pairs={{0,64},{16,80},{32,96},{48,112},{64,0},{80,16},{96,32},{112,48},{1... | collective-permute-start | bytes 1572872 | tf_op jit(solution)/shard_map/zl/ppermute | solution.py:314
  40.9 12.7 %collective-permute-start.3 = (bf16[64,2,16,128]{3,2,1,0:T(8,128)(2,1)S(1)}, bf16[64,2,16,128]{3,2,1,0:T(8,128)(2,1)S(1)}, u32[]{:S(2)}, u32[]{:S(2)}) collective-permute-start(bf16[64,2,16,128]{3,2,1,0:T(8,128)(2,1)S(1)} %bitcast.37), channel_id=1, source_target_pairs={{0,48},{16,0},{32,16},{48,32},{64,112},{80,64},{96,80},{112,96},{1... | collective-permute-start | bytes 1572872 | tf_op jit(solution)/shard_map/y_above/ppermute | solution.py:314
  41.6 13.0 %collective-permute-start = (bf16[64,2,16,128]{3,2,1,0:T(8,128)(2,1)S(1)}, bf16[64,2,16,128]{3,2,1,0:T(8,128)(2,1)S(1)}, u32[]{:S(2)}, u32[]{:S(2)}) collective-permute-start(bf16[64,2,16,128]{3,2,1,0:T(8,128)(2,1)S(1)} %bitcast.38), channel_id=1, source_target_pairs={{0,16},{16,32},{32,48},{48,0},{64,80},{80,96},{96,112},{112,64},{1... | collective-permute-start | bytes 1572872 | tf_op jit(solution)/shard_map/y_below/ppermute | solution.py:314
  42.4 15.8 %collective-permute-start.13 = (bf16[64,2,16,128]{3,2,1,0:T(8,128)(2,1)S(1)}, bf16[64,2,16,128]{3,2,1,0:T(8,128)(2,1)}, u32[]{:S(2)}, u32[]{:S(2)}) collective-permute-start(bf16[64,2,16,128]{3,2,1,0:T(8,128)(2,1)S(1)} %bitcast.39), channel_id=1, source_target_pairs={{0,6},{1,7},{2,0},{3,1},{4,2},{5,3},{6,4},{7,5},{8,14},{9,15},{10,... | collective-permute-start | bytes 1572872 | tf_op jit(solution)/shard_map/x_above/ppermute | solution.py:318
  43.5 17.4 %collective-permute-start.10 = (bf16[64,2,16,128]{3,2,1,0:T(8,128)(2,1)S(1)}, bf16[64,2,16,128]{3,2,1,0:T(8,128)(2,1)}, u32[]{:S(2)}, u32[]{:S(2)}) collective-permute-start(bf16[64,2,16,128]{3,2,1,0:T(8,128)(2,1)S(1)} %bitcast.40), channel_id=1, source_target_pairs={{0,2},{1,3},{2,4},{3,5},{4,6},{5,7},{6,0},{7,1},{8,10},{9,11},{10,... | collective-permute-start | bytes 1572872 | tf_op jit(solution)/shard_map/x_below/ppermute | solution.py:318
  52.8 11.5 %collective-permute-start.5 = (bf16[64,2,16,128]{3,2,1,0:T(8,128)(2,1)S(1)}, bf16[64,2,16,128]{3,2,1,0:T(8,128)(2,1)}, u32[]{:S(2)}, u32[]{:S(2)}) collective-permute-start(bf16[64,2,16,128]{3,2,1,0:T(8,128)(2,1)S(1)} %collective-permute-done.1.refs_1_.refs_7_), channel_id=1, source_target_pairs={{0,48},{16,0},{32,16},{48,32},{64,112},{80,64},{96,80},{112,96},{1... | collective-permute-start | bytes 1572872 | tf_op jit(solution)/shard_map/zl_above/ppermute | solution.py:314
  53.6 12.6 %collective-permute-start.2 = (bf16[64,2,16,128]{3,2,1,0:T(8,128)(2,1)S(1)}, bf16[64,2,16,128]{3,2,1,0:T(8,128)(2,1)S(1)}, u32[]{:S(2)}, u32[]{:S(2)}) collective-permute-start(bf16[64,2,16,128]{3,2,1,0:T(8,128)(2,1)S(1)} %collective-permute-done.1.refs_1_.refs_7_), channel_id=1, source_target_pairs={{0,16},{16,32},{32,48},{48,0},{64,80},{80,96},{96,112},{112,64},{1... | collective-permute-start | bytes 1572872 | tf_op jit(solution)/shard_map/zl_below/ppermute | solution.py:314
  55.5 20.6 %collective-permute-start.7 = (bf16[64,2,16,128]{3,2,1,0:T(8,128)(2,1)}, bf16[64,2,16,128]{3,2,1,0:T(8,128)(2,1)S(1)}, u32[]{:S(2)}, u32[]{:S(2)}) collective-permute-start(bf16[64,2,16,128]{3,2,1,0:T(8,128)(2,1)} %shard_map.58.refs_0_), channel_id=1, source_target_pairs={{0,8},{1,9},{2,10},{3,11},{4,12},{5,13},{6,14},{7,15},{8,0},{9,1},... | collective-permute-start | bytes 1572872 | tf_op jit(solution)/shard_map/zh/ppermute | solution.py:318
  58.2 14.4 %collective-permute-start.14 = (bf16[64,2,16,128]{3,2,1,0:T(8,128)(2,1)}, bf16[64,2,16,128]{3,2,1,0:T(8,128)(2,1)S(1)}, u32[]{:S(2)}, u32[]{:S(2)}) collective-permute-start(bf16[64,2,16,128]{3,2,1,0:T(8,128)(2,1)} %collective-permute-done.13.refs_2_), channel_id=1, source_target_pairs={{0,7},{1,6},{2,1},{3,0},{4,3},{5,2},{6,5},{7,4},{8,15},{9,14},{10,... | collective-permute-start | bytes 1572872 | tf_op jit(solution)/shard_map/x_far_other/ppermute | solution.py:318
  60.9 15.2 %collective-permute-start.11 = (bf16[64,2,16,128]{3,2,1,0:T(8,128)(2,1)}, bf16[64,2,16,128]{3,2,1,0:T(8,128)(2,1)}, u32[]{:S(2)}, u32[]{:S(2)}) collective-permute-start(bf16[64,2,16,128]{3,2,1,0:T(8,128)(2,1)} %collective-permute-done.10.refs_1_), channel_id=1, source_target_pairs={{0,2},{1,3},{2,4},{3,5},{4,6},{5,7},{6,0},{7,1},{8,10},{9,11},{10,... | collective-permute-start | bytes 1572872 | tf_op jit(solution)/shard_map/x_far/ppermute | solution.py:318
  64.4 11.7 %collective-permute-start.6 = (bf16[64,2,16,128]{3,2,1,0:T(8,128)(2,1)}, bf16[64,2,16,128]{3,2,1,0:T(8,128)(2,1)S(1)}, u32[]{:S(2)}, u32[]{:S(2)}) collective-permute-start(bf16[64,2,16,128]{3,2,1,0:T(8,128)(2,1)} %collective-permute-done.5.refs_9_), channel_id=1, source_target_pairs={{0,48},{16,0},{32,16},{48,32},{64,112},{80,64},{96,80},{112,96},{1... | collective-permute-start | bytes 1572872 | tf_op jit(solution)/shard_map/zl_far/ppermute | solution.py:314
  67.0 11.7 %collective-permute-start.4 = (bf16[64,2,16,128]{3,2,1,0:T(8,128)(2,1)}, bf16[64,2,16,128]{3,2,1,0:T(8,128)(2,1)S(1)}, u32[]{:S(2)}, u32[]{:S(2)}) collective-permute-start(bf16[64,2,16,128]{3,2,1,0:T(8,128)(2,1)} %shard_map.57.refs_4_), channel_id=1, source_target_pairs={{0,16},{16,32},{32,48},{48,0},{64,80},{80,96},{96,112},{112,64},{1... | collective-permute-start | bytes 1572872 | tf_op jit(solution)/shard_map/y_far/ppermute | solution.py:314
  79.5 8.5 %collective-permute-start.15 = (bf16[64,2,16,128]{3,2,1,0:T(8,128)(2,1)}, bf16[64,2,16,128]{3,2,1,0:T(8,128)(2,1)S(1)}, u32[]{:S(2)}, u32[]{:S(2)}) collective-permute-start(bf16[64,2,16,128]{3,2,1,0:T(8,128)(2,1)} %get-tuple-element.28), channel_id=1, source_target_pairs={{0,1},{1,0},{2,3},{3,2},{4,5},{5,4},{6,7},{7,6},{8,9},{9,8},{10,11... | collective-permute-start | bytes 1572872 | tf_op jit(solution)/shard_map/core_swap/ppermute | solution.py:318
  83.6 5.8 %collective-permute-start.16 = (bf16[64,2,16,128]{3,2,1,0:T(8,128)(2,1)}, bf16[64,2,16,128]{3,2,1,0:T(8,128)(2,1)S(1)}, u32[]{:S(2)}, u32[]{:S(2)}) collective-permute-start(bf16[64,2,16,128]{3,2,1,0:T(8,128)(2,1)} %get-tuple-element.26.refs_12_), channel_id=1, source_target_pairs={{0,1},{1,0},{2,3},{3,2},{4,5},{5,4},{6,7},{7,6},{8,9},{9,8},{10,11... | collective-permute-start | bytes 1572872 | tf_op jit(solution)/shard_map/core_swap/ppermute | solution.py:318
  83.6 5.8 %collective-permute-start.17 = (bf16[64,2,16,128]{3,2,1,0:T(8,128)(2,1)}, bf16[64,2,16,128]{3,2,1,0:T(8,128)(2,1)S(1)}, u32[]{:S(2)}, u32[]{:S(2)}) collective-permute-start(bf16[64,2,16,128]{3,2,1,0:T(8,128)(2,1)} %get-tuple-element.27.refs_13_), channel_id=1, source_target_pairs={{0,1},{1,0},{2,3},{3,2},{4,5},{5,4},{6,7},{7,6},{8,9},{9,8},{10,11... | collective-permute-start | bytes 1572872 | tf_op jit(solution)/shard_map/core_swap/ppermute | solution.py:318
  84.1 24.0 %collective-permute-start.12 = (bf16[64,2,16,128]{3,2,1,0:T(8,128)(2,1)}, bf16[64,2,16,128]{3,2,1,0:T(8,128)(2,1)S(1)}, u32[]{:S(2)}, u32[]{:S(2)}) collective-permute-start(bf16[64,2,16,128]{3,2,1,0:T(8,128)(2,1)} %collective-permute-done.11.refs_6_.refs_14_), channel_id=1, source_target_pairs={{0,8},{1,9},{2,10},{3,11},{4,12},{5,13},{6,14},{7,15},{8,0},{9,1},... | collective-permute-start | bytes 1572872 | tf_op jit(solution)/shard_map/zh_far/ppermute | solution.py:318
  87.9 20.2 %collective-permute-start.9 = (bf16[64,2,16,128]{3,2,1,0:T(8,128)(2,1)}, bf16[64,2,16,128]{3,2,1,0:T(8,128)(2,1)S(1)}, u32[]{:S(2)}, u32[]{:S(2)}) collective-permute-start(bf16[64,2,16,128]{3,2,1,0:T(8,128)(2,1)} %copy-done.4), channel_id=1, source_target_pairs={{0,6},{1,7},{2,0},{3,1},{4,2},{5,3},{6,4},{7,5},{8,14},{9,15},{10,... | collective-permute-start | bytes 1572872 | tf_op jit(solution)/shard_map/zh_above/ppermute | solution.py:318
  88.0 20.2 %collective-permute-start.8 = (bf16[64,2,16,128]{3,2,1,0:T(8,128)(2,1)}, bf16[64,2,16,128]{3,2,1,0:T(8,128)(2,1)S(1)}, u32[]{:S(2)}, u32[]{:S(2)}) collective-permute-start(bf16[64,2,16,128]{3,2,1,0:T(8,128)(2,1)} %copy-done.4), channel_id=1, source_target_pairs={{0,2},{1,3},{2,4},{3,5},{4,6},{5,7},{6,0},{7,1},{8,10},{9,11},{10,... | collective-permute-start | bytes 1572872 | tf_op jit(solution)/shard_map/zh_below/ppermute | solution.py:318
  109.9 2.6 %collective-permute-start.18 = (bf16[64,2,16,128]{3,2,1,0:T(8,128)(2,1)}, bf16[64,2,16,128]{3,2,1,0:T(8,128)(2,1)S(1)}, u32[]{:S(2)}, u32[]{:S(2)}) collective-permute-start(bf16[64,2,16,128]{3,2,1,0:T(8,128)(2,1)} %get-tuple-element.29.refs_11_), channel_id=1, source_target_pairs={{0,1},{1,0},{2,3},{3,2},{4,5},{5,4},{6,7},{7,6},{8,9},{9,8},{10,11... | collective-permute-start | bytes 1572872 | tf_op jit(solution)/shard_map/core_swap/ppermute | solution.py:318
  110.8 2.5 %collective-permute-start.19 = (bf16[64,2,16,128]{3,2,1,0:T(8,128)(2,1)}, bf16[64,2,16,128]{3,2,1,0:T(8,128)(2,1)S(1)}, u32[]{:S(2)}, u32[]{:S(2)}) collective-permute-start(bf16[64,2,16,128]{3,2,1,0:T(8,128)(2,1)} %get-tuple-element.30.refs_12_), channel_id=1, source_target_pairs={{0,1},{1,0},{2,3},{3,2},{4,5},{5,4},{6,7},{7,6},{8,9},{9,8},{10,11... | collective-permute-start | bytes 1572872 | tf_op jit(solution)/shard_map/core_swap/ppermute | solution.py:318
  110.8 3.2 %collective-permute-start.20 = (bf16[64,2,16,128]{3,2,1,0:T(8,128)(2,1)}, bf16[64,2,16,128]{3,2,1,0:T(8,128)(2,1)S(1)}, u32[]{:S(2)}, u32[]{:S(2)}) collective-permute-start(bf16[64,2,16,128]{3,2,1,0:T(8,128)(2,1)} %get-tuple-element.31.refs_13_), channel_id=1, source_target_pairs={{0,1},{1,0},{2,3},{3,2},{4,5},{5,4},{6,7},{7,6},{8,9},{9,8},{10,11... | collective-permute-start | bytes 1572872 | tf_op jit(solution)/shard_map/core_swap/ppermute | solution.py:318
  111.3 3.5 %collective-permute-start.21 = (bf16[64,2,16,128]{3,2,1,0:T(8,128)(2,1)}, bf16[64,2,16,128]{3,2,1,0:T(8,128)(2,1)S(1)}, u32[]{:S(2)}, u32[]{:S(2)}) collective-permute-start(bf16[64,2,16,128]{3,2,1,0:T(8,128)(2,1)} %get-tuple-element.32.refs_14_), channel_id=1, source_target_pairs={{0,1},{1,0},{2,3},{3,2},{4,5},{5,4},{6,7},{7,6},{8,9},{9,8},{10,11... | collective-permute-start | bytes 1572872 | tf_op jit(solution)/shard_map/core_swap/ppermute | solution.py:318
  (20 other events, 29.6 us)
where the time goes:
time: 133 us
  Pallas kernels  41.7 us (31%)
  waiting for transfers between devices  38.9 us (29%)
  starting transfers between devices  35.2 us (26%)
  local copies, waits for them, and re-layouts  15 us (11%)
    pallas_call x2, Pallas kernels, pair_chunk(): pl.pallas_call(kernel, out_shape=jax.ShapeDtypeStruct((256, 128, 2 * MAX_...  33.8 us
    ppermute x15, starting transfers between devices, along_col(): return lax.ppermute(block, 'col', perm)  18.8 us
    ppermute x7, waiting for transfers between devices, along_row(): return lax.ppermute(block, 'row', perm)  14.9 us
    ppermute x15, waiting for transfers between devices, along_col(): return lax.ppermute(block, 'col', perm)  12.6 us
    all_to_all x1, starting transfers between devices, per_device(): lax.all_to_all(ordered.reshape(128, GROUP, SLICE), ('row', 'col'), split_...  11.5 us
    all_to_all x1, waiting for transfers between devices, per_device(): lax.all_to_all(ordered.reshape(128, GROUP, SLICE), ('row', 'col'), split_...  11.4 us
    unnamed x43, local copies, waits for them, and re-layouts  9.84 us
    ppermute x7, starting transfers between devices, along_row(): return lax.ppermute(block, 'row', perm)  4.97 us
  transfers between devices with their start and end apart: 23, of which 12 were waited for; matrix products, arithmetic and copies ran while one was open for 6% of the time, Pallas kernels for 13%

commit v1 on v0

--- a/solution.py
+++ b/solution.py
@@ -331,7 +331,7 @@
     y_far, zl_far = along_row(y_below, y_up, "y_far"), along_row(zl_above, y_down, "zl_far")
     zh_below, zh_above = along_col(zh, x_up, "zh_below"), along_col(zh, x_down, "zh_above")
     zh_far = along_col(x_far, col_perm(1, 0, 0), "zh_far")
-    again, x_below, x_above = after([again, x_below, x_above], [y_far, zl_far, zh, x_far, x_far_other])
+    again, x_below, x_above = after([again, x_below, x_above], [zl_below, zl_above, zh, x_far, x_far_other])
     swaps = [along_col(block, flip, "core_swap") for block in (again, x_below, x_above)]
 
     second = [own, y_below, y_above, y_far, zl, zl_below, zl_above, zl_far]

time: 133 us -> 131 us (0.985)
  starting transfers between devices: 35.2 us -> 33.5 us
    ppermute x15, waiting for transfers between devices: 12.6 us -> 7.34 us  [along_col(): return lax.ppermute(block, 'col', perm)]
    ppermute x7, waiting for transfers between devices: 14.9 us -> 19.7 us  [along_row(): return lax.ppermute(block, 'row', perm)]
    ppermute x15, starting transfers between devices: 18.8 us -> 16.2 us  [along_col(): return lax.ppermute(block, 'col', perm)]
where the time goes in v1:
time: 131 us
  Pallas kernels  41.7 us (32%)
  waiting for transfers between devices  38.5 us (29%)
  starting transfers between devices  33.5 us (26%)
  local copies, waits for them, and re-layouts  15.1 us (12%)
    pallas_call x2, Pallas kernels, pair_chunk(): pl.pallas_call(kernel, out_shape=jax.ShapeDtypeStruct((256, 128, 2 * MAX_...  33.8 us
    ppermute x7, waiting for transfers between devices, along_row(): return lax.ppermute(block, 'row', perm)  19.7 us
    ppermute x15, starting transfers between devices, along_col(): return lax.ppermute(block, 'col', perm)  16.2 us
    all_to_all x1, starting transfers between devices, per_device(): lax.all_to_all(ordered.reshape(128, GROUP, SLICE), ('row', 'col'), split_...  11.5 us
    all_to_all x1, waiting for transfers between devices, per_device(): lax.all_to_all(ordered.reshape(128, GROUP, SLICE), ('row', 'col'), split_...  11.4 us
    unnamed x43, local copies, waits for them, and re-layouts  9.97 us
    ppermute x15, waiting for transfers between devices, along_col(): return lax.ppermute(block, 'col', perm)  7.34 us
    ppermute x7, starting transfers between devices, along_row(): return lax.ppermute(block, 'row', perm)  5.84 us
  transfers between devices with their start and end apart: 23, of which 12 were waited for; matrix products, arithmetic and copies ran while one was open for 6% of the time, Pallas kernels for 13%

profile of v1, /device:TPU:1, one launch (start us, length us, event | category | flops | bytes accessed | tf_op | source)
XLA Modules:
  0.0 130.5 jit_solution(12265780913311733818)
XLA Ops:
  0.0 4.2 %shard_map.55 = bf16[2048,150]{1,0:T(8,128)(2,1)} custom-call(s32[1,2048]{1,0:T(1,128)} %bitcast.48, bf16[150,2048]{1,0:T(8,128)(2,1)} %bitcast.45), custom_call_target="tpu_custom_call" | custom-call | tf_op jit(solution)/shard_map/pallas_call | solution.py:63
  4.2 11.5 %all-to-all-start = ((bf16[128,16,150]{2,1,0:T(8,128)(2,1)}), bf16[128,16,150]{2,1,0:T(8,128)(2,1)S(1)}, u32[]{:S(2)}, u32[]{:S(2)}) async-start(bf16[128,16,150]{2,1,0:T(8,128)(2,1)} %bitcast.44), calls=%async_computation | async-start | bytes 2097152 | tf_op jit(solution)/shard_map/all_to_all | solution.py:289
  17.6 1.3 copy.18
  22.4 0.9 fusion.refs_1_
  23.3 11.4 %all-to-all-done.x_ref = bf16[128,16,150]{2,1,0:T(8,128)(2,1)S(1)} async-done(((bf16[128,16,150]{2,1,0:T(8,128)(2,1)}), bf16[128,16,150]{2,1,0:T(8,128)(2,1)S(1)}, u32[]{:S(2)}, u32[]{:S(2)}) %all-to-all-start) | async-done | bytes 614432 | tf_op jit(solution)/shard_map/all_to_all | solution.py:289
  34.9 1.1 copy-done.1
  36.0 3.7 %shard_map.56 = (bf16[2048,128]{1,0:T(8,128)(2,1)S(1)}, bf16[2048,128]{1,0:T(8,128)(2,1)S(1)}) custom-call(bf16[128,16,150]{2,1,0:T(8,128)(2,1)S(1)} %all-to-all-done.x_ref, f32[512,1]{1,0:T(8,128)S(1)} %copy.20.keep_ref, bf16[4,150,512]{2,1,0:T(8,128)(2,1)S(1)} %copy-done.1), custom_call_target="tpu_custom_call" | custom-call | tf_op jit(solution)/shard_map/pallas_call | solution.py:117
  40.9 1.2 collective-permute-start.13
  42.4 0.9 collective-permute-start.3
  43.8 9.0 %collective-permute-done.1.refs_1_.refs_7_ = bf16[64,2,16,128]{3,2,1,0:T(8,128)(2,1)S(1)} collective-permute-done((bf16[64,2,16,128]{3,2,1,0:T(8,128)(2,1)S(1)}, bf16[64,2,16,128]{3,2,1,0:T(8,128)(2,1)S(1)}, u32[]{:S(2)}, u32[]{:S(2)}) %collective-permute-start.1) | collective-permute-done | bytes 524320 | tf_op jit(solution)/shard_map/zl/ppermute | solution.py:314
  54.3 1.0 collective-permute-done.10.refs_1_
  55.3 3.0 %collective-permute-start.14 = (bf16[64,2,16,128]{3,2,1,0:T(8,128)(2,1)}, bf16[64,2,16,128]{3,2,1,0:T(8,128)(2,1)}, u32[]{:S(2)}, u32[]{:S(2)}) collective-permute-start(bf16[64,2,16,128]{3,2,1,0:T(8,128)(2,1)} %collective-permute-done.13.refs_2_), channel_id=1, source_target_pairs={{0,7},{1,6},{2,1},{3,0},{4,3},{5,2},{6,5},{7,4},{8,15},{9,14},{10,... | collective-permute-start | bytes 1572872 | tf_op jit(solution)/shard_map/x_far_other/ppermute | solution.py:318
  59.9 0.9 collective-permute-start.7
  60.9 7.3 %collective-permute-done.2.refs_1_.refs_3_.refs_8_ = bf16[64,2,16,128]{3,2,1,0:T(8,128)(2,1)S(1)} collective-permute-done((bf16[64,2,16,128]{3,2,1,0:T(8,128)(2,1)S(1)}, bf16[64,2,16,128]{3,2,1,0:T(8,128)(2,1)S(1)}, u32[]{:S(2)}, u32[]{:S(2)}) %collective-permute-start.2) | collective-permute-done | bytes 524320 | tf_op jit(solution)/shard_map/zl_below/ppermute | solution.py:314
  69.0 2.7 %collective-permute-start.6 = (bf16[64,2,16,128]{3,2,1,0:T(8,128)(2,1)S(1)}, bf16[64,2,16,128]{3,2,1,0:T(8,128)(2,1)S(1)}, u32[]{:S(2)}, u32[]{:S(2)}) collective-permute-start(bf16[64,2,16,128]{3,2,1,0:T(8,128)(2,1)S(1)} %collective-permute-done.5.refs_4_.refs_9_), channel_id=1, source_target_pairs={{0,48},{16,0},{32,16},{48,32},{64,112},{80,64},{96,80},{112,96},{1... | collective-permute-start | bytes 1572872 | tf_op jit(solution)/shard_map/zl_far/ppermute | solution.py:314
  71.7 2.0 %collective-permute-done.11.refs_6_.refs_14_ = bf16[64,2,16,128]{3,2,1,0:T(8,128)(2,1)} collective-permute-done((bf16[64,2,16,128]{3,2,1,0:T(8,128)(2,1)}, bf16[64,2,16,128]{3,2,1,0:T(8,128)(2,1)}, u32[]{:S(2)}, u32[]{:S(2)}) %collective-permute-start.11) | collective-permute-done | bytes 524320 | tf_op jit(solution)/shard_map/x_far/ppermute | solution.py:318
  75.2 1.6 %collective-permute-start.15 = (bf16[64,2,16,128]{3,2,1,0:T(8,128)(2,1)}, bf16[64,2,16,128]{3,2,1,0:T(8,128)(2,1)S(1)}, u32[]{:S(2)}, u32[]{:S(2)}) collective-permute-start(bf16[64,2,16,128]{3,2,1,0:T(8,128)(2,1)} %get-tuple-element.28), channel_id=1, source_target_pairs={{0,1},{1,0},{2,3},{3,2},{4,5},{5,4},{6,7},{7,6},{8,9},{9,8},{10,11... | collective-permute-start | bytes 1572872 | tf_op jit(solution)/shard_map/core_swap/ppermute | solution.py:318
  77.3 3.4 %collective-permute-done.6.refs_10_ = bf16[64,2,16,128]{3,2,1,0:T(8,128)(2,1)S(1)} collective-permute-done((bf16[64,2,16,128]{3,2,1,0:T(8,128)(2,1)S(1)}, bf16[64,2,16,128]{3,2,1,0:T(8,128)(2,1)S(1)}, u32[]{:S(2)}, u32[]{:S(2)}) %collective-permute-start.6) | collective-permute-done | bytes 524320 | tf_op jit(solution)/shard_map/zl_far/ppermute | solution.py:314
  80.7 2.2 %collective-permute-start.12 = (bf16[64,2,16,128]{3,2,1,0:T(8,128)(2,1)}, bf16[64,2,16,128]{3,2,1,0:T(8,128)(2,1)S(1)}, u32[]{:S(2)}, u32[]{:S(2)}) collective-permute-start(bf16[64,2,16,128]{3,2,1,0:T(8,128)(2,1)} %collective-permute-done.11.refs_6_.refs_14_), channel_id=1, source_target_pairs={{0,8},{1,9},{2,10},{3,11},{4,12},{5,13},{6,14},{7,15},{8,0},{9,1},... | collective-permute-start | bytes 1572872 | tf_op jit(solution)/shard_map/zh_far/ppermute | solution.py:318
  82.9 2.4 %collective-permute-start.9 = (bf16[64,2,16,128]{3,2,1,0:T(8,128)(2,1)}, bf16[64,2,16,128]{3,2,1,0:T(8,128)(2,1)S(1)}, u32[]{:S(2)}, u32[]{:S(2)}) collective-permute-start(bf16[64,2,16,128]{3,2,1,0:T(8,128)(2,1)} %copy-done.5), channel_id=1, source_target_pairs={{0,6},{1,7},{2,0},{3,1},{4,2},{5,3},{6,4},{7,5},{8,14},{9,15},{10,... | collective-permute-start | bytes 1572872 | tf_op jit(solution)/shard_map/zh_above/ppermute | solution.py:318
  87.1 17.1 %shard_map.60.refs_4_.refs_19_ = bf16[256,128,256]{2,1,0:T(8,128)(2,1)} custom-call(s32[16]{0:T(128)} %stack.114.refs_0_, f32[256,128]{1,0:T(8,128)} %fusion.refs_1_, bf16[256,512]{1,0:T(8,128)(2,1)} %constant.178.refs_2_, bf16[64,2,16,128]{3,2,1,0:T(8,128)(2,1)} %bitcast.41, bf16[64,2,16,128]{3,2,1,0:T(8,128)(2,1)} %shard_map.57.refs_4_, ...), custom_call_target="tpu_custom_call" | custom-call | flops 15000000512 | bytes 10485760 | tf_op jit(solution)/shard_map/pallas_call | solution.py:243
  106.0 2.8 %collective-permute-start.18 = (bf16[64,2,16,128]{3,2,1,0:T(8,128)(2,1)}, bf16[64,2,16,128]{3,2,1,0:T(8,128)(2,1)S(1)}, u32[]{:S(2)}, u32[]{:S(2)}) collective-permute-start(bf16[64,2,16,128]{3,2,1,0:T(8,128)(2,1)} %get-tuple-element.29.refs_11_), channel_id=1, source_target_pairs={{0,1},{1,0},{2,3},{3,2},{4,5},{5,4},{6,7},{7,6},{8,9},{9,8},{10,11... | collective-permute-start | bytes 1572872 | tf_op jit(solution)/shard_map/core_swap/ppermute | solution.py:318
  109.3 1.2 collective-permute-done.18.refs_15_
  113.6 16.7 %shard_map.62 = bf16[256,128,256]{2,1,0:T(8,128)(2,1)} custom-call(s32[16]{0:T(128)} %stack.123.refs_0_, f32[256,128]{1,0:T(8,128)} %fusion.refs_1_, bf16[256,512]{1,0:T(8,128)(2,1)} %constant.178.refs_2_, bf16[64,2,16,128]{3,2,1,0:T(8,128)(2,1)} %bitcast.43, bf16[64,2,16,128]{3,2,1,0:T(8,128)(2,1)} %shard_map.57.refs_4_, ...), custom_call_target="tpu_custom_call", output_to_operand_aliasing={{}: (19, {})} | custom-call | flops 15000000512 | bytes 10485760 | tf_op jit(solution)/shard_map/pallas_call | solution.py:243
  (95 shorter events, 20.3 us)
Async XLA Ops:
  4.2 30.6 %all-to-all-start = ((bf16[128,16,150]{2,1,0:T(8,128)(2,1)}), bf16[128,16,150]{2,1,0:T(8,128)(2,1)S(1)}, u32[]{:S(2)}, u32[]{:S(2)}) async-start(bf16[128,16,150]{2,1,0:T(8,128)(2,1)} %bitcast.44), calls=%async_computation | async-start | bytes 2097152 | tf_op jit(solution)/shard_map/all_to_all | solution.py:289
  40.5 44.8 %copy-start.2 = (bf16[2048,128]{1,0:T(8,128)(2,1)}, bf16[2048,128]{1,0:T(8,128)(2,1)S(1)}, u32[]{:S(2)}) copy-start(bf16[2048,128]{1,0:T(8,128)(2,1)S(1)} %get-tuple-element.23) | copy-start | bytes 1572868
  40.5 12.3 %collective-permute-start.1 = (bf16[64,2,16,128]{3,2,1,0:T(8,128)(2,1)S(1)}, bf16[64,2,16,128]{3,2,1,0:T(8,128)(2,1)S(1)}, u32[]{:S(2)}, u32[]{:S(2)}) collective-permute-start(bf16[64,2,16,128]{3,2,1,0:T(8,128)(2,1)S(1)} %bitcast.36), channel_id=1, source_target_pairs={{0,64},{16,80},{32,96},{48,112},{64,0},{80,16},{96,32},{112,48},{1... | collective-permute-start | bytes 1572872 | tf_op jit(solution)/shard_map/zl/ppermute | solution.py:314
  40.9 12.7 %collective-permute-start.13 = (bf16[64,2,16,128]{3,2,1,0:T(8,128)(2,1)S(1)}, bf16[64,2,16,128]{3,2,1,0:T(8,128)(2,1)}, u32[]{:S(2)}, u32[]{:S(2)}) collective-permute-start(bf16[64,2,16,128]{3,2,1,0:T(8,128)(2,1)S(1)} %bitcast.37), channel_id=1, source_target_pairs={{0,6},{1,7},{2,0},{3,1},{4,2},{5,3},{6,4},{7,5},{8,14},{9,15},{10,... | collective-permute-start | bytes 1572872 | tf_op jit(solution)/shard_map/x_above/ppermute | solution.py:318
  42.1 13.2 %collective-permute-start.10 = (bf16[64,2,16,128]{3,2,1,0:T(8,128)(2,1)S(1)}, bf16[64,2,16,128]{3,2,1,0:T(8,128)(2,1)}, u32[]{:S(2)}, u32[]{:S(2)}) collective-permute-start(bf16[64,2,16,128]{3,2,1,0:T(8,128)(2,1)S(1)} %bitcast.38), channel_id=1, source_target_pairs={{0,2},{1,3},{2,4},{3,5},{4,6},{5,7},{6,0},{7,1},{8,10},{9,11},{10,... | collective-permute-start | bytes 1572872 | tf_op jit(solution)/shard_map/x_below/ppermute | solution.py:318
  42.4 16.0 %collective-permute-start.3 = (bf16[64,2,16,128]{3,2,1,0:T(8,128)(2,1)S(1)}, bf16[64,2,16,128]{3,2,1,0:T(8,128)(2,1)S(1)}, u32[]{:S(2)}, u32[]{:S(2)}) collective-permute-start(bf16[64,2,16,128]{3,2,1,0:T(8,128)(2,1)S(1)} %bitcast.39), channel_id=1, source_target_pairs={{0,48},{16,0},{32,16},{48,32},{64,112},{80,64},{96,80},{112,96},{1... | collective-permute-start | bytes 1572872 | tf_op jit(solution)/shard_map/y_above/ppermute | solution.py:314
  43.3 15.8 %collective-permute-start = (bf16[64,2,16,128]{3,2,1,0:T(8,128)(2,1)S(1)}, bf16[64,2,16,128]{3,2,1,0:T(8,128)(2,1)S(1)}, u32[]{:S(2)}, u32[]{:S(2)}) collective-permute-start(bf16[64,2,16,128]{3,2,1,0:T(8,128)(2,1)S(1)} %bitcast.40), channel_id=1, source_target_pairs={{0,16},{16,32},{32,48},{48,0},{64,80},{80,96},{96,112},{112,64},{1... | collective-permute-start | bytes 1572872 | tf_op jit(solution)/shard_map/y_below/ppermute | solution.py:314
  52.8 16.1 %collective-permute-start.5 = (bf16[64,2,16,128]{3,2,1,0:T(8,128)(2,1)S(1)}, bf16[64,2,16,128]{3,2,1,0:T(8,128)(2,1)S(1)}, u32[]{:S(2)}, u32[]{:S(2)}) collective-permute-start(bf16[64,2,16,128]{3,2,1,0:T(8,128)(2,1)S(1)} %collective-permute-done.1.refs_1_.refs_7_), channel_id=1, source_target_pairs={{0,48},{16,0},{32,16},{48,32},{64,112},{80,64},{96,80},{112,96},{1... | collective-permute-start | bytes 1572872 | tf_op jit(solution)/shard_map/zl_above/ppermute | solution.py:314
  53.6 14.6 %collective-permute-start.2 = (bf16[64,2,16,128]{3,2,1,0:T(8,128)(2,1)S(1)}, bf16[64,2,16,128]{3,2,1,0:T(8,128)(2,1)S(1)}, u32[]{:S(2)}, u32[]{:S(2)}) collective-permute-start(bf16[64,2,16,128]{3,2,1,0:T(8,128)(2,1)S(1)} %collective-permute-done.1.refs_1_.refs_7_), channel_id=1, source_target_pairs={{0,16},{16,32},{32,48},{48,0},{64,80},{80,96},{96,112},{112,64},{1... | collective-permute-start | bytes 1572872 | tf_op jit(solution)/shard_map/zl_below/ppermute | solution.py:314
  55.3 16.4 %collective-permute-start.14 = (bf16[64,2,16,128]{3,2,1,0:T(8,128)(2,1)}, bf16[64,2,16,128]{3,2,1,0:T(8,128)(2,1)}, u32[]{:S(2)}, u32[]{:S(2)}) collective-permute-start(bf16[64,2,16,128]{3,2,1,0:T(8,128)(2,1)} %collective-permute-done.13.refs_2_), channel_id=1, source_target_pairs={{0,7},{1,6},{2,1},{3,0},{4,3},{5,2},{6,5},{7,4},{8,15},{9,14},{10,... | collective-permute-start | bytes 1572872 | tf_op jit(solution)/shard_map/x_far_other/ppermute | solution.py:318
  58.3 15.3 %collective-permute-start.11 = (bf16[64,2,16,128]{3,2,1,0:T(8,128)(2,1)}, bf16[64,2,16,128]{3,2,1,0:T(8,128)(2,1)}, u32[]{:S(2)}, u32[]{:S(2)}) collective-permute-start(bf16[64,2,16,128]{3,2,1,0:T(8,128)(2,1)} %collective-permute-done.10.refs_1_), channel_id=1, source_target_pairs={{0,2},{1,3},{2,4},{3,5},{4,6},{5,7},{6,0},{7,1},{8,10},{9,11},{10,... | collective-permute-start | bytes 1572872 | tf_op jit(solution)/shard_map/x_far/ppermute | solution.py:318
  59.9 14.5 %collective-permute-start.7 = (bf16[64,2,16,128]{3,2,1,0:T(8,128)(2,1)}, bf16[64,2,16,128]{3,2,1,0:T(8,128)(2,1)S(1)}, u32[]{:S(2)}, u32[]{:S(2)}) collective-permute-start(bf16[64,2,16,128]{3,2,1,0:T(8,128)(2,1)} %shard_map.58.refs_0_), channel_id=1, source_target_pairs={{0,8},{1,9},{2,10},{3,11},{4,12},{5,13},{6,14},{7,15},{8,0},{9,1},... | collective-permute-start | bytes 1572872 | tf_op jit(solution)/shard_map/zh/ppermute | solution.py:318
  69.0 13.9 %collective-permute-start.4 = (bf16[64,2,16,128]{3,2,1,0:T(8,128)(2,1)}, bf16[64,2,16,128]{3,2,1,0:T(8,128)(2,1)S(1)}, u32[]{:S(2)}, u32[]{:S(2)}) collective-permute-start(bf16[64,2,16,128]{3,2,1,0:T(8,128)(2,1)} %shard_map.57.refs_4_), channel_id=1, source_target_pairs={{0,16},{16,32},{32,48},{48,0},{64,80},{80,96},{96,112},{112,64},{1... | collective-permute-start | bytes 1572872 | tf_op jit(solution)/shard_map/y_far/ppermute | solution.py:314
  69.0 11.7 %collective-permute-start.6 = (bf16[64,2,16,128]{3,2,1,0:T(8,128)(2,1)S(1)}, bf16[64,2,16,128]{3,2,1,0:T(8,128)(2,1)S(1)}, u32[]{:S(2)}, u32[]{:S(2)}) collective-permute-start(bf16[64,2,16,128]{3,2,1,0:T(8,128)(2,1)S(1)} %collective-permute-done.5.refs_4_.refs_9_), channel_id=1, source_target_pairs={{0,48},{16,0},{32,16},{48,32},{64,112},{80,64},{96,80},{112,96},{1... | collective-permute-start | bytes 1572872 | tf_op jit(solution)/shard_map/zl_far/ppermute | solution.py:314
  75.2 10.1 %collective-permute-start.15 = (bf16[64,2,16,128]{3,2,1,0:T(8,128)(2,1)}, bf16[64,2,16,128]{3,2,1,0:T(8,128)(2,1)S(1)}, u32[]{:S(2)}, u32[]{:S(2)}) collective-permute-start(bf16[64,2,16,128]{3,2,1,0:T(8,128)(2,1)} %get-tuple-element.28), channel_id=1, source_target_pairs={{0,1},{1,0},{2,3},{3,2},{4,5},{5,4},{6,7},{7,6},{8,9},{9,8},{10,11... | collective-permute-start | bytes 1572872 | tf_op jit(solution)/shard_map/core_swap/ppermute | solution.py:318
  76.8 8.5 %collective-permute-start.16 = (bf16[64,2,16,128]{3,2,1,0:T(8,128)(2,1)}, bf16[64,2,16,128]{3,2,1,0:T(8,128)(2,1)S(1)}, u32[]{:S(2)}, u32[]{:S(2)}) collective-permute-start(bf16[64,2,16,128]{3,2,1,0:T(8,128)(2,1)} %get-tuple-element.26.refs_12_), channel_id=1, source_target_pairs={{0,1},{1,0},{2,3},{3,2},{4,5},{5,4},{6,7},{7,6},{8,9},{9,8},{10,11... | collective-permute-start | bytes 1572872 | tf_op jit(solution)/shard_map/core_swap/ppermute | solution.py:318
  76.8 8.6 %collective-permute-start.17 = (bf16[64,2,16,128]{3,2,1,0:T(8,128)(2,1)}, bf16[64,2,16,128]{3,2,1,0:T(8,128)(2,1)S(1)}, u32[]{:S(2)}, u32[]{:S(2)}) collective-permute-start(bf16[64,2,16,128]{3,2,1,0:T(8,128)(2,1)} %get-tuple-element.27.refs_13_), channel_id=1, source_target_pairs={{0,1},{1,0},{2,3},{3,2},{4,5},{5,4},{6,7},{7,6},{8,9},{9,8},{10,11... | collective-permute-start | bytes 1572872 | tf_op jit(solution)/shard_map/core_swap/ppermute | solution.py:318
  80.7 23.5 %collective-permute-start.12 = (bf16[64,2,16,128]{3,2,1,0:T(8,128)(2,1)}, bf16[64,2,16,128]{3,2,1,0:T(8,128)(2,1)S(1)}, u32[]{:S(2)}, u32[]{:S(2)}) collective-permute-start(bf16[64,2,16,128]{3,2,1,0:T(8,128)(2,1)} %collective-permute-done.11.refs_6_.refs_14_), channel_id=1, source_target_pairs={{0,8},{1,9},{2,10},{3,11},{4,12},{5,13},{6,14},{7,15},{8,0},{9,1},... | collective-permute-start | bytes 1572872 | tf_op jit(solution)/shard_map/zh_far/ppermute | solution.py:318
  82.9 21.3 %collective-permute-start.9 = (bf16[64,2,16,128]{3,2,1,0:T(8,128)(2,1)}, bf16[64,2,16,128]{3,2,1,0:T(8,128)(2,1)S(1)}, u32[]{:S(2)}, u32[]{:S(2)}) collective-permute-start(bf16[64,2,16,128]{3,2,1,0:T(8,128)(2,1)} %copy-done.5), channel_id=1, source_target_pairs={{0,6},{1,7},{2,0},{3,1},{4,2},{5,3},{6,4},{7,5},{8,14},{9,15},{10,... | collective-permute-start | bytes 1572872 | tf_op jit(solution)/shard_map/zh_above/ppermute | solution.py:318
  85.3 18.9 %collective-permute-start.8 = (bf16[64,2,16,128]{3,2,1,0:T(8,128)(2,1)}, bf16[64,2,16,128]{3,2,1,0:T(8,128)(2,1)S(1)}, u32[]{:S(2)}, u32[]{:S(2)}) collective-permute-start(bf16[64,2,16,128]{3,2,1,0:T(8,128)(2,1)} %copy-done.5), channel_id=1, source_target_pairs={{0,2},{1,3},{2,4},{3,5},{4,6},{5,7},{6,0},{7,1},{8,10},{9,11},{10,... | collective-permute-start | bytes 1572872 | tf_op jit(solution)/shard_map/zh_below/ppermute | solution.py:318
  106.0 4.5 %collective-permute-start.18 = (bf16[64,2,16,128]{3,2,1,0:T(8,128)(2,1)}, bf16[64,2,16,128]{3,2,1,0:T(8,128)(2,1)S(1)}, u32[]{:S(2)}, u32[]{:S(2)}) collective-permute-start(bf16[64,2,16,128]{3,2,1,0:T(8,128)(2,1)} %get-tuple-element.29.refs_11_), channel_id=1, source_target_pairs={{0,1},{1,0},{2,3},{3,2},{4,5},{5,4},{6,7},{7,6},{8,9},{9,8},{10,11... | collective-permute-start | bytes 1572872 | tf_op jit(solution)/shard_map/core_swap/ppermute | solution.py:318
  108.7 2.5 %collective-permute-start.19 = (bf16[64,2,16,128]{3,2,1,0:T(8,128)(2,1)}, bf16[64,2,16,128]{3,2,1,0:T(8,128)(2,1)S(1)}, u32[]{:S(2)}, u32[]{:S(2)}) collective-permute-start(bf16[64,2,16,128]{3,2,1,0:T(8,128)(2,1)} %get-tuple-element.30.refs_12_), channel_id=1, source_target_pairs={{0,1},{1,0},{2,3},{3,2},{4,5},{5,4},{6,7},{7,6},{8,9},{9,8},{10,11... | collective-permute-start | bytes 1572872 | tf_op jit(solution)/shard_map/core_swap/ppermute | solution.py:318
  108.8 3.2 %collective-permute-start.20 = (bf16[64,2,16,128]{3,2,1,0:T(8,128)(2,1)}, bf16[64,2,16,128]{3,2,1,0:T(8,128)(2,1)S(1)}, u32[]{:S(2)}, u32[]{:S(2)}) collective-permute-start(bf16[64,2,16,128]{3,2,1,0:T(8,128)(2,1)} %get-tuple-element.31.refs_13_), channel_id=1, source_target_pairs={{0,1},{1,0},{2,3},{3,2},{4,5},{5,4},{6,7},{7,6},{8,9},{9,8},{10,11... | collective-permute-start | bytes 1572872 | tf_op jit(solution)/shard_map/core_swap/ppermute | solution.py:318
  109.3 3.5 %collective-permute-start.21 = (bf16[64,2,16,128]{3,2,1,0:T(8,128)(2,1)}, bf16[64,2,16,128]{3,2,1,0:T(8,128)(2,1)S(1)}, u32[]{:S(2)}, u32[]{:S(2)}) collective-permute-start(bf16[64,2,16,128]{3,2,1,0:T(8,128)(2,1)} %get-tuple-element.32.refs_14_), channel_id=1, source_target_pairs={{0,1},{1,0},{2,3},{3,2},{4,5},{5,4},{6,7},{7,6},{8,9},{9,8},{10,11... | collective-permute-start | bytes 1572872 | tf_op jit(solution)/shard_map/core_swap/ppermute | solution.py:318
  (20 other events, 32.0 us)

commit v2 on v1

--- a/solution.py
+++ b/solution.py
@@ -126,6 +126,19 @@
     return [out.reshape(KGS, 2, GROUP, 128) for out in outs]
 
 
+def bring_in(table):
+    def kernel(in_ref, out_ref):
+        out_ref[...] = in_ref[...]
+
+    return pl.pallas_call(
+        kernel,
+        out_shape=jax.ShapeDtypeStruct(table.shape, table.dtype),
+        in_specs=[vmem],
+        out_specs=vmem,
+        compiler_params=pltpu.CompilerParams(vmem_limit_bytes=20 * 2**20),
+    )(table)
+
+
 def after(arrays, others):
     count = len(arrays)
     return pl.pallas_call(
@@ -303,8 +316,9 @@
         ).astype(jnp.int32)
         for dz in range(2)
     ]
-    slices, keep, scale, places = lax.optimization_barrier((slices, keep, scale, places))
-    own, again = whiten(slices, keep, forward_table())
+    forward = bring_in(forward_table())
+    slices, keep, scale, places, forward = lax.optimization_barrier((slices, keep, scale, places, forward))
+    own, again = whiten(slices, keep, forward)
 
     y_up, y_down = row_perm(0, 1), row_perm(0, -1)
     x_up, x_down, flip = col_perm(0, 1, 0), col_perm(0, -1, 0), col_perm(0, 0, 1)
@@ -329,10 +343,11 @@
 
     (y_below,) = after([y_below], [zl_below])
     y_far, zl_far = along_row(y_below, y_up, "y_far"), along_row(zl_above, y_down, "zl_far")
+    again, x_below, x_above = after([again, x_below, x_above], [zl_below, zl_above, zh, x_far, x_far_other])
+    swaps = [along_col(block, flip, "core_swap") for block in (again, x_below, x_above)]
+    zh, x_far = after([zh, x_far], swaps)
     zh_below, zh_above = along_col(zh, x_up, "zh_below"), along_col(zh, x_down, "zh_above")
     zh_far = along_col(x_far, col_perm(1, 0, 0), "zh_far")
-    again, x_below, x_above = after([again, x_below, x_above], [zl_below, zl_above, zh, x_far, x_far_other])
-    swaps = [along_col(block, flip, "core_swap") for block in (again, x_below, x_above)]
 
     second = [own, y_below, y_above, y_far, zl, zl_below, zl_above, zl_far]
     table = lag_table()

time: 131 us -> 135 us (1.031)
  waiting for transfers between devices: 38.5 us -> 43.4 us
  starting transfers between devices: 33.5 us -> 29 us
  local copies, waits for them, and re-layouts: 15.1 us -> 18.1 us
    ppermute x15, waiting for transfers between devices: 7.34 us -> 19.4 us  [along_col(): return lax.ppermute(block, 'col', perm)]
    all_to_all x1, waiting for transfers between devices: 11.4 us -> 5.73 us  [per_device(): lax.all_to_all(ordered.reshape(128, GROUP, SLICE), ('row', 'col'), split_...]
    ppermute x15, starting transfers between devices: 16.2 us -> 12.8 us  [along_col(): return lax.ppermute(block, 'col', perm)]
    ppermute x7, waiting for transfers between devices: 19.7 us -> 18.3 us  [along_row(): return lax.ppermute(block, 'row', perm)]
  transfers between devices with their start and end apart: 23 -> 23, of which waited for: 12 -> 15; matrix products, arithmetic and copies ran while one was open for 6% -> 9% of each run, Pallas kernels for 13% -> 13%
where the time goes in v2:
time: 135 us
  waiting for transfers between devices  43.4 us (32%)
  Pallas kernels  41.7 us (31%)
  starting transfers between devices  29 us (21%)
  local copies, waits for them, and re-layouts  18.1 us (13%)
    pallas_call x2, Pallas kernels, pair_chunk(): pl.pallas_call(kernel, out_shape=jax.ShapeDtypeStruct((256, 128, 2 * MAX_...  33.7 us
    ppermute x15, waiting for transfers between devices, along_col(): return lax.ppermute(block, 'col', perm)  19.4 us
    ppermute x7, waiting for transfers between devices, along_row(): return lax.ppermute(block, 'row', perm)  18.3 us
    ppermute x15, starting transfers between devices, along_col(): return lax.ppermute(block, 'col', perm)  12.8 us
    all_to_all x1, starting transfers between devices, per_device(): lax.all_to_all(ordered.reshape(128, GROUP, SLICE), ('row', 'col'), split_...  11.5 us
    unnamed x43, local copies, waits for them, and re-layouts  9.38 us
    all_to_all x1, waiting for transfers between devices, per_device(): lax.all_to_all(ordered.reshape(128, GROUP, SLICE), ('row', 'col'), split_...  5.73 us
    ppermute x7, starting transfers between devices, along_row(): return lax.ppermute(block, 'row', perm)  4.62 us
  transfers between devices with their start and end apart: 23, of which 15 were waited for; matrix products, arithmetic and copies ran while one was open for 9% of the time, Pallas kernels for 13%

profile of v2, /device:TPU:1, one launch (start us, length us, event | category | flops | bytes accessed | tf_op | source)
XLA Modules:
  0.0 134.8 jit_solution(2870341632211393339)
XLA Ops:
  0.0 4.2 %shard_map.55 = bf16[2048,150]{1,0:T(8,128)(2,1)} custom-call(s32[1,2048]{1,0:T(1,128)} %bitcast.48, bf16[150,2048]{1,0:T(8,128)(2,1)} %bitcast.45), custom_call_target="tpu_custom_call" | custom-call | tf_op jit(solution)/shard_map/pallas_call | solution.py:63
  4.2 11.5 %all-to-all-start = ((bf16[128,16,150]{2,1,0:T(8,128)(2,1)}), bf16[128,16,150]{2,1,0:T(8,128)(2,1)S(1)}, u32[]{:S(2)}, u32[]{:S(2)}) async-start(bf16[128,16,150]{2,1,0:T(8,128)(2,1)} %bitcast.44), calls=%async_computation | async-start | bytes 2097152 | tf_op jit(solution)/shard_map/all_to_all | solution.py:302
  17.6 1.1 copy-done.1
  18.7 1.3 copy.20
  20.0 1.0 convert_element_type.9
  21.1 1.8 %gather_fusion = f32[16,32]{1,0:T(8,128)S(1)} fusion(f32[32,2048]{0,1:T(8,128)} %convert_element_type.9, s32[1024]{0:T(1024)S(1)} %pad_clamp_fusion.3), kind=kCustom, calls=%fused_computation | custom fusion | bytes 4160 | tf_op jit(solution)/shard_map/jit(_take)/gather | solution.py:309
  23.0 1.9 %gather_fusion.3 = f32[128,32]{1,0:T(8,128)S(1)} fusion(f32[32,2048]{0,1:T(8,128)} %convert_element_type.9, s32[1024]{0:T(1024)S(1)} %pad_clamp_fusion), kind=kCustom, calls=%fused_computation.3 | custom fusion | bytes 33280 | tf_op jit(solution)/shard_map/jit(_take)/gather | solution.py:308
  24.9 1.9 %gather_fusion.1 = f32[256,32]{1,0:T(8,128)S(1)} fusion(f32[32,2048]{0,1:T(8,128)} %convert_element_type.9, s32[1024]{0:T(1024)S(1)} %pad_clamp_fusion.2), kind=kCustom, calls=%fused_computation.1 | custom fusion | bytes 66560 | tf_op jit(solution)/shard_map/jit(_take)/gather | solution.py:307
  29.0 5.7 %all-to-all-done.x_ref = bf16[128,16,150]{2,1,0:T(8,128)(2,1)S(1)} async-done(((bf16[128,16,150]{2,1,0:T(8,128)(2,1)}), bf16[128,16,150]{2,1,0:T(8,128)(2,1)S(1)}, u32[]{:S(2)}, u32[]{:S(2)}) %all-to-all-start) | async-done | bytes 614432 | tf_op jit(solution)/shard_map/all_to_all | solution.py:302
  34.9 3.8 %shard_map.57 = (bf16[2048,128]{1,0:T(8,128)(2,1)S(1)}, bf16[2048,128]{1,0:T(8,128)(2,1)S(1)}) custom-call(bf16[128,16,150]{2,1,0:T(8,128)(2,1)S(1)} %all-to-all-done.x_ref, f32[512,1]{1,0:T(8,128)S(1)} %copy.22.keep_ref, bf16[4,150,512]{2,1,0:T(8,128)(2,1)S(1)} %shard_map.56.f_ref), custom_call_target="tpu_custom_call" | custom-call | tf_op jit(solution)/shard_map/pallas_call | solution.py:117
  39.9 1.2 collective-permute-start.10
  42.8 9.0 %collective-permute-done.1.refs_1_.refs_7_ = bf16[64,2,16,128]{3,2,1,0:T(8,128)(2,1)S(1)} collective-permute-done((bf16[64,2,16,128]{3,2,1,0:T(8,128)(2,1)S(1)}, bf16[64,2,16,128]{3,2,1,0:T(8,128)(2,1)S(1)}, u32[]{:S(2)}, u32[]{:S(2)}) %collective-permute-start.1) | collective-permute-done | bytes 524320 | tf_op jit(solution)/shard_map/zl/ppermute | solution.py:328
  54.2 3.0 %collective-permute-start.11 = (bf16[64,2,16,128]{3,2,1,0:T(8,128)(2,1)}, bf16[64,2,16,128]{3,2,1,0:T(8,128)(2,1)}, u32[]{:S(2)}, u32[]{:S(2)}) collective-permute-start(bf16[64,2,16,128]{3,2,1,0:T(8,128)(2,1)} %collective-permute-done.10.refs_2_), channel_id=1, source_target_pairs={{0,7},{1,6},{2,1},{3,0},{4,3},{5,2},{6,5},{7,4},{8,15},{9,14},{10,... | collective-permute-start | bytes 1572872 | tf_op jit(solution)/shard_map/x_far_other/ppermute | solution.py:332
  59.8 9.1 %collective-permute-done.11.refs_7_.refs_18_ = bf16[64,2,16,128]{3,2,1,0:T(8,128)(2,1)} collective-permute-done((bf16[64,2,16,128]{3,2,1,0:T(8,128)(2,1)}, bf16[64,2,16,128]{3,2,1,0:T(8,128)(2,1)}, u32[]{:S(2)}, u32[]{:S(2)}) %collective-permute-start.11) | collective-permute-done | bytes 524320 | tf_op jit(solution)/shard_map/x_far_other/ppermute | solution.py:332
  68.9 3.7 %collective-permute-done.9.refs_6_.refs_1_ = bf16[64,2,16,128]{3,2,1,0:T(8,128)(2,1)S(1)} collective-permute-done((bf16[64,2,16,128]{3,2,1,0:T(8,128)(2,1)}, bf16[64,2,16,128]{3,2,1,0:T(8,128)(2,1)S(1)}, u32[]{:S(2)}, u32[]{:S(2)}) %collective-permute-start.9) | collective-permute-done | bytes 524320 | tf_op jit(solution)/shard_map/x_far/ppermute | solution.py:332
  74.4 1.3 %collective-permute-start.12 = (bf16[64,2,16,128]{3,2,1,0:T(8,128)(2,1)}, bf16[64,2,16,128]{3,2,1,0:T(8,128)(2,1)S(1)}, u32[]{:S(2)}, u32[]{:S(2)}) collective-permute-start(bf16[64,2,16,128]{3,2,1,0:T(8,128)(2,1)} %get-tuple-element.29), channel_id=1, source_target_pairs={{0,1},{1,0},{2,3},{3,2},{4,5},{5,4},{6,7},{7,6},{8,9},{9,8},{10,11... | collective-permute-start | bytes 1572872 | tf_op jit(solution)/shard_map/core_swap/ppermute | solution.py:332
  76.3 1.3 collective-permute-start.6
  79.8 2.4 %collective-permute-start.16 = (bf16[64,2,16,128]{3,2,1,0:T(8,128)(2,1)}, bf16[64,2,16,128]{3,2,1,0:T(8,128)(2,1)S(1)}, u32[]{:S(2)}, u32[]{:S(2)}) collective-permute-start(bf16[64,2,16,128]{3,2,1,0:T(8,128)(2,1)} %get-tuple-element.32.refs_0_), channel_id=1, source_target_pairs={{0,6},{1,7},{2,0},{3,1},{4,2},{5,3},{6,4},{7,5},{8,14},{9,15},{10,... | collective-permute-start | bytes 1572872 | tf_op jit(solution)/shard_map/zh_above/ppermute | solution.py:332
  82.9 7.2 %collective-permute-done.6.refs_10_ = bf16[64,2,16,128]{3,2,1,0:T(8,128)(2,1)S(1)} collective-permute-done((bf16[64,2,16,128]{3,2,1,0:T(8,128)(2,1)}, bf16[64,2,16,128]{3,2,1,0:T(8,128)(2,1)S(1)}, u32[]{:S(2)}, u32[]{:S(2)}) %collective-permute-start.6) | collective-permute-done | bytes 524320 | tf_op jit(solution)/shard_map/zl_far/ppermute | solution.py:328
  90.0 2.1 %collective-permute-done.4.refs_6_ = bf16[64,2,16,128]{3,2,1,0:T(8,128)(2,1)S(1)} collective-permute-done((bf16[64,2,16,128]{3,2,1,0:T(8,128)(2,1)}, bf16[64,2,16,128]{3,2,1,0:T(8,128)(2,1)S(1)}, u32[]{:S(2)}, u32[]{:S(2)}) %collective-permute-start.4) | collective-permute-done | bytes 524320 | tf_op jit(solution)/shard_map/y_far/ppermute | solution.py:328
  92.9 17.0 %shard_map.62.refs_4_.refs_19_ = bf16[256,128,256]{2,1,0:T(8,128)(2,1)} custom-call(s32[16]{0:T(128)} %stack.114.refs_0_, f32[256,128]{1,0:T(8,128)} %fusion.refs_1_, bf16[256,512]{1,0:T(8,128)(2,1)} %constant.178.refs_2_, bf16[64,2,16,128]{3,2,1,0:T(8,128)(2,1)} %bitcast.41, bf16[64,2,16,128]{3,2,1,0:T(8,128)(2,1)} %shard_map.58.refs_4_, ...), custom_call_target="tpu_custom_call" | custom-call | flops 15000000512 | bytes 10485760 | tf_op jit(solution)/shard_map/pallas_call | solution.py:256
  111.8 1.3 collective-permute-start.18
  113.5 1.2 collective-permute-done.18.refs_15_
  117.9 16.7 %shard_map.64 = bf16[256,128,256]{2,1,0:T(8,128)(2,1)} custom-call(s32[16]{0:T(128)} %stack.123.refs_0_, f32[256,128]{1,0:T(8,128)} %fusion.refs_1_, bf16[256,512]{1,0:T(8,128)(2,1)} %constant.178.refs_2_, bf16[64,2,16,128]{3,2,1,0:T(8,128)(2,1)} %bitcast.43, bf16[64,2,16,128]{3,2,1,0:T(8,128)(2,1)} %shard_map.58.refs_4_, ...), custom_call_target="tpu_custom_call", output_to_operand_aliasing={{}: (19, {})} | custom-call | flops 15000000512 | bytes 10485760 | tf_op jit(solution)/shard_map/pallas_call | solution.py:256
  (97 shorter events, 23.5 us)
Async XLA Ops:
  4.2 30.6 %all-to-all-start = ((bf16[128,16,150]{2,1,0:T(8,128)(2,1)}), bf16[128,16,150]{2,1,0:T(8,128)(2,1)S(1)}, u32[]{:S(2)}, u32[]{:S(2)}) async-start(bf16[128,16,150]{2,1,0:T(8,128)(2,1)} %bitcast.44), calls=%async_computation | async-start | bytes 2097152 | tf_op jit(solution)/shard_map/all_to_all | solution.py:302
  39.5 52.6 %copy-start.2 = (bf16[2048,128]{1,0:T(8,128)(2,1)}, bf16[2048,128]{1,0:T(8,128)(2,1)S(1)}, u32[]{:S(2)}) copy-start(bf16[2048,128]{1,0:T(8,128)(2,1)S(1)} %get-tuple-element.27) | copy-start | bytes 1572868
  39.5 12.3 %collective-permute-start.1 = (bf16[64,2,16,128]{3,2,1,0:T(8,128)(2,1)S(1)}, bf16[64,2,16,128]{3,2,1,0:T(8,128)(2,1)S(1)}, u32[]{:S(2)}, u32[]{:S(2)}) collective-permute-start(bf16[64,2,16,128]{3,2,1,0:T(8,128)(2,1)S(1)} %bitcast.36), channel_id=1, source_target_pairs={{0,64},{16,80},{32,96},{48,112},{64,0},{80,16},{96,32},{112,48},{1... | collective-permute-start | bytes 1572872 | tf_op jit(solution)/shard_map/zl/ppermute | solution.py:328
  39.9 12.7 %collective-permute-start.10 = (bf16[64,2,16,128]{3,2,1,0:T(8,128)(2,1)S(1)}, bf16[64,2,16,128]{3,2,1,0:T(8,128)(2,1)}, u32[]{:S(2)}, u32[]{:S(2)}) collective-permute-start(bf16[64,2,16,128]{3,2,1,0:T(8,128)(2,1)S(1)} %bitcast.37), channel_id=1, source_target_pairs={{0,6},{1,7},{2,0},{3,1},{4,2},{5,3},{6,4},{7,5},{8,14},{9,15},{10,... | collective-permute-start | bytes 1572872 | tf_op jit(solution)/shard_map/x_above/ppermute | solution.py:332
  41.0 13.2 %collective-permute-start.8 = (bf16[64,2,16,128]{3,2,1,0:T(8,128)(2,1)S(1)}, bf16[64,2,16,128]{3,2,1,0:T(8,128)(2,1)}, u32[]{:S(2)}, u32[]{:S(2)}) collective-permute-start(bf16[64,2,16,128]{3,2,1,0:T(8,128)(2,1)S(1)} %bitcast.38), channel_id=1, source_target_pairs={{0,2},{1,3},{2,4},{3,5},{4,6},{5,7},{6,0},{7,1},{8,10},{9,11},{10,... | collective-permute-start | bytes 1572872 | tf_op jit(solution)/shard_map/x_below/ppermute | solution.py:332
  41.3 16.0 %collective-permute-start.3 = (bf16[64,2,16,128]{3,2,1,0:T(8,128)(2,1)S(1)}, bf16[64,2,16,128]{3,2,1,0:T(8,128)(2,1)S(1)}, u32[]{:S(2)}, u32[]{:S(2)}) collective-permute-start(bf16[64,2,16,128]{3,2,1,0:T(8,128)(2,1)S(1)} %bitcast.39), channel_id=1, source_target_pairs={{0,48},{16,0},{32,16},{48,32},{64,112},{80,64},{96,80},{112,96},{1... | collective-permute-start | bytes 1572872 | tf_op jit(solution)/shard_map/y_above/ppermute | solution.py:328
  42.3 15.8 %collective-permute-start = (bf16[64,2,16,128]{3,2,1,0:T(8,128)(2,1)S(1)}, bf16[64,2,16,128]{3,2,1,0:T(8,128)(2,1)S(1)}, u32[]{:S(2)}, u32[]{:S(2)}) collective-permute-start(bf16[64,2,16,128]{3,2,1,0:T(8,128)(2,1)S(1)} %bitcast.40), channel_id=1, source_target_pairs={{0,16},{16,32},{32,48},{48,0},{64,80},{80,96},{96,112},{112,64},{1... | collective-permute-start | bytes 1572872 | tf_op jit(solution)/shard_map/y_below/ppermute | solution.py:328
  51.8 20.8 %collective-permute-start.5 = (bf16[64,2,16,128]{3,2,1,0:T(8,128)(2,1)S(1)}, bf16[64,2,16,128]{3,2,1,0:T(8,128)(2,1)}, u32[]{:S(2)}, u32[]{:S(2)}) collective-permute-start(bf16[64,2,16,128]{3,2,1,0:T(8,128)(2,1)S(1)} %collective-permute-done.1.refs_1_.refs_7_), channel_id=1, source_target_pairs={{0,48},{16,0},{32,16},{48,32},{64,112},{80,64},{96,80},{112,96},{1... | collective-permute-start | bytes 1572872 | tf_op jit(solution)/shard_map/zl_above/ppermute | solution.py:328
  52.5 20.1 %collective-permute-start.2 = (bf16[64,2,16,128]{3,2,1,0:T(8,128)(2,1)S(1)}, bf16[64,2,16,128]{3,2,1,0:T(8,128)(2,1)S(1)}, u32[]{:S(2)}, u32[]{:S(2)}) collective-permute-start(bf16[64,2,16,128]{3,2,1,0:T(8,128)(2,1)S(1)} %collective-permute-done.1.refs_1_.refs_7_), channel_id=1, source_target_pairs={{0,16},{16,32},{32,48},{48,0},{64,80},{80,96},{96,112},{112,64},{1... | collective-permute-start | bytes 1572872 | tf_op jit(solution)/shard_map/zl_below/ppermute | solution.py:328
  54.2 14.7 %collective-permute-start.11 = (bf16[64,2,16,128]{3,2,1,0:T(8,128)(2,1)}, bf16[64,2,16,128]{3,2,1,0:T(8,128)(2,1)}, u32[]{:S(2)}, u32[]{:S(2)}) collective-permute-start(bf16[64,2,16,128]{3,2,1,0:T(8,128)(2,1)} %collective-permute-done.10.refs_2_), channel_id=1, source_target_pairs={{0,7},{1,6},{2,1},{3,0},{4,3},{5,2},{6,5},{7,4},{8,15},{9,14},{10,... | collective-permute-start | bytes 1572872 | tf_op jit(solution)/shard_map/x_far_other/ppermute | solution.py:332
  57.3 15.3 %collective-permute-start.9 = (bf16[64,2,16,128]{3,2,1,0:T(8,128)(2,1)}, bf16[64,2,16,128]{3,2,1,0:T(8,128)(2,1)S(1)}, u32[]{:S(2)}, u32[]{:S(2)}) collective-permute-start(bf16[64,2,16,128]{3,2,1,0:T(8,128)(2,1)} %collective-permute-done.8.refs_1_), channel_id=1, source_target_pairs={{0,2},{1,3},{2,4},{3,5},{4,6},{5,7},{6,0},{7,1},{8,10},{9,11},{10,... | collective-permute-start | bytes 1572872 | tf_op jit(solution)/shard_map/x_far/ppermute | solution.py:332
  58.9 14.5 %collective-permute-start.7 = (bf16[64,2,16,128]{3,2,1,0:T(8,128)(2,1)}, bf16[64,2,16,128]{3,2,1,0:T(8,128)(2,1)S(1)}, u32[]{:S(2)}, u32[]{:S(2)}) collective-permute-start(bf16[64,2,16,128]{3,2,1,0:T(8,128)(2,1)} %shard_map.59.refs_0_), channel_id=1, source_target_pairs={{0,8},{1,9},{2,10},{3,11},{4,12},{5,13},{6,14},{7,15},{8,0},{9,1},... | collective-permute-start | bytes 1572872 | tf_op jit(solution)/shard_map/zh/ppermute | solution.py:332
  74.4 3.3 %collective-permute-start.12 = (bf16[64,2,16,128]{3,2,1,0:T(8,128)(2,1)}, bf16[64,2,16,128]{3,2,1,0:T(8,128)(2,1)S(1)}, u32[]{:S(2)}, u32[]{:S(2)}) collective-permute-start(bf16[64,2,16,128]{3,2,1,0:T(8,128)(2,1)} %get-tuple-element.29), channel_id=1, source_target_pairs={{0,1},{1,0},{2,3},{3,2},{4,5},{5,4},{6,7},{7,6},{8,9},{9,8},{10,11... | collective-permute-start | bytes 1572872 | tf_op jit(solution)/shard_map/core_swap/ppermute | solution.py:332
  75.7 2.5 %collective-permute-start.13 = (bf16[64,2,16,128]{3,2,1,0:T(8,128)(2,1)}, bf16[64,2,16,128]{3,2,1,0:T(8,128)(2,1)S(1)}, u32[]{:S(2)}, u32[]{:S(2)}) collective-permute-start(bf16[64,2,16,128]{3,2,1,0:T(8,128)(2,1)} %get-tuple-element.30.refs_12_), channel_id=1, source_target_pairs={{0,1},{1,0},{2,3},{3,2},{4,5},{5,4},{6,7},{7,6},{8,9},{9,8},{10,11... | collective-permute-start | bytes 1572872 | tf_op jit(solution)/shard_map/core_swap/ppermute | solution.py:332
  75.7 3.2 %collective-permute-start.14 = (bf16[64,2,16,128]{3,2,1,0:T(8,128)(2,1)}, bf16[64,2,16,128]{3,2,1,0:T(8,128)(2,1)S(1)}, u32[]{:S(2)}, u32[]{:S(2)}) collective-permute-start(bf16[64,2,16,128]{3,2,1,0:T(8,128)(2,1)} %get-tuple-element.31.refs_13_), channel_id=1, source_target_pairs={{0,1},{1,0},{2,3},{3,2},{4,5},{5,4},{6,7},{7,6},{8,9},{9,8},{10,11... | collective-permute-start | bytes 1572872 | tf_op jit(solution)/shard_map/core_swap/ppermute | solution.py:332
  76.3 13.8 %collective-permute-start.6 = (bf16[64,2,16,128]{3,2,1,0:T(8,128)(2,1)}, bf16[64,2,16,128]{3,2,1,0:T(8,128)(2,1)S(1)}, u32[]{:S(2)}, u32[]{:S(2)}) collective-permute-start(bf16[64,2,16,128]{3,2,1,0:T(8,128)(2,1)} %collective-permute-done.5.refs_4_.refs_9_), channel_id=1, source_target_pairs={{0,48},{16,0},{32,16},{48,32},{64,112},{80,64},{96,80},{112,96},{1... | collective-permute-start | bytes 1572872 | tf_op jit(solution)/shard_map/zl_far/ppermute | solution.py:328
  77.6 14.5 %collective-permute-start.4 = (bf16[64,2,16,128]{3,2,1,0:T(8,128)(2,1)}, bf16[64,2,16,128]{3,2,1,0:T(8,128)(2,1)S(1)}, u32[]{:S(2)}, u32[]{:S(2)}) collective-permute-start(bf16[64,2,16,128]{3,2,1,0:T(8,128)(2,1)} %shard_map.58.refs_4_), channel_id=1, source_target_pairs={{0,16},{16,32},{32,48},{48,0},{64,80},{80,96},{96,112},{112,64},{1... | collective-permute-start | bytes 1572872 | tf_op jit(solution)/shard_map/y_far/ppermute | solution.py:328
  79.8 30.1 %collective-permute-start.16 = (bf16[64,2,16,128]{3,2,1,0:T(8,128)(2,1)}, bf16[64,2,16,128]{3,2,1,0:T(8,128)(2,1)S(1)}, u32[]{:S(2)}, u32[]{:S(2)}) collective-permute-start(bf16[64,2,16,128]{3,2,1,0:T(8,128)(2,1)} %get-tuple-element.32.refs_0_), channel_id=1, source_target_pairs={{0,6},{1,7},{2,0},{3,1},{4,2},{5,3},{6,4},{7,5},{8,14},{9,15},{10,... | collective-permute-start | bytes 1572872 | tf_op jit(solution)/shard_map/zh_above/ppermute | solution.py:332
  82.2 27.7 %collective-permute-start.15 = (bf16[64,2,16,128]{3,2,1,0:T(8,128)(2,1)}, bf16[64,2,16,128]{3,2,1,0:T(8,128)(2,1)S(1)}, u32[]{:S(2)}, u32[]{:S(2)}) collective-permute-start(bf16[64,2,16,128]{3,2,1,0:T(8,128)(2,1)} %get-tuple-element.32.refs_0_), channel_id=1, source_target_pairs={{0,2},{1,3},{2,4},{3,5},{4,6},{5,7},{6,0},{7,1},{8,10},{9,11},{10,... | collective-permute-start | bytes 1572872 | tf_op jit(solution)/shard_map/zh_below/ppermute | solution.py:332
  82.2 27.7 %collective-permute-start.17 = (bf16[64,2,16,128]{3,2,1,0:T(8,128)(2,1)}, bf16[64,2,16,128]{3,2,1,0:T(8,128)(2,1)S(1)}, u32[]{:S(2)}, u32[]{:S(2)}) collective-permute-start(bf16[64,2,16,128]{3,2,1,0:T(8,128)(2,1)} %get-tuple-element.33.refs_14_), channel_id=1, source_target_pairs={{0,8},{1,9},{2,10},{3,11},{4,12},{5,13},{6,14},{7,15},{8,0},{9,1},... | collective-permute-start | bytes 1572872 | tf_op jit(solution)/shard_map/zh_far/ppermute | solution.py:332
  111.8 3.0 %collective-permute-start.18 = (bf16[64,2,16,128]{3,2,1,0:T(8,128)(2,1)}, bf16[64,2,16,128]{3,2,1,0:T(8,128)(2,1)S(1)}, u32[]{:S(2)}, u32[]{:S(2)}) collective-permute-start(bf16[64,2,16,128]{3,2,1,0:T(8,128)(2,1)} %get-tuple-element.35.refs_11_), channel_id=1, source_target_pairs={{0,1},{1,0},{2,3},{3,2},{4,5},{5,4},{6,7},{7,6},{8,9},{9,8},{10,11... | collective-permute-start | bytes 1572872 | tf_op jit(solution)/shard_map/core_swap/ppermute | solution.py:332
  113.0 2.5 %collective-permute-start.19 = (bf16[64,2,16,128]{3,2,1,0:T(8,128)(2,1)}, bf16[64,2,16,128]{3,2,1,0:T(8,128)(2,1)S(1)}, u32[]{:S(2)}, u32[]{:S(2)}) collective-permute-start(bf16[64,2,16,128]{3,2,1,0:T(8,128)(2,1)} %get-tuple-element.36.refs_12_), channel_id=1, source_target_pairs={{0,1},{1,0},{2,3},{3,2},{4,5},{5,4},{6,7},{7,6},{8,9},{9,8},{10,11... | collective-permute-start | bytes 1572872 | tf_op jit(solution)/shard_map/core_swap/ppermute | solution.py:332
  113.0 3.2 %collective-permute-start.20 = (bf16[64,2,16,128]{3,2,1,0:T(8,128)(2,1)}, bf16[64,2,16,128]{3,2,1,0:T(8,128)(2,1)S(1)}, u32[]{:S(2)}, u32[]{:S(2)}) collective-permute-start(bf16[64,2,16,128]{3,2,1,0:T(8,128)(2,1)} %get-tuple-element.37.refs_13_), channel_id=1, source_target_pairs={{0,1},{1,0},{2,3},{3,2},{4,5},{5,4},{6,7},{7,6},{8,9},{9,8},{10,11... | collective-permute-start | bytes 1572872 | tf_op jit(solution)/shard_map/core_swap/ppermute | solution.py:332
  113.5 3.5 %collective-permute-start.21 = (bf16[64,2,16,128]{3,2,1,0:T(8,128)(2,1)}, bf16[64,2,16,128]{3,2,1,0:T(8,128)(2,1)S(1)}, u32[]{:S(2)}, u32[]{:S(2)}) collective-permute-start(bf16[64,2,16,128]{3,2,1,0:T(8,128)(2,1)} %get-tuple-element.38.refs_14_), channel_id=1, source_target_pairs={{0,1},{1,0},{2,3},{3,2},{4,5},{5,4},{6,7},{7,6},{8,9},{9,8},{10,11... | collective-permute-start | bytes 1572872 | tf_op jit(solution)/shard_map/core_swap/ppermute | solution.py:332
  (20 other events, 26.2 us)
